TPU v7x, 32 devices: a whole 2x2x4 slice. The times are simulated.
32 devices in a mesh: seq: 4 (over z), ch: 8 (over y, x, core).
Axes of the slice: x: 2, y: 2, z: 4, core: 2. Of those that a mesh axis runs over, the one named last changes fastest.
Arguments:
- proj: bfloat16 [4, 2048, 3, 8192], P(None, ('seq', 'ch')), may hold values from -6 to 6
- short_w: float32 [3, 3, 8192], P(None, None, 'ch'), may hold values from -3.5 to 3.5
- long_filter: bfloat16 [512, 2048], P('ch'), may hold values from -1 to 1
Outputs:
- hyena_out: bfloat16 [4, 2048, 8192], P(None, ('seq', 'ch'))
All inputs are finite; a program needn't handle non-finite values.
Results may differ from a plain program's by a relative error of at most 0.0085.
Values may be sent and summed in bfloat16 or wider, within the bound.
No kernel may reach another device: no remote copies, remote signals or barrier semaphores. Data moves between devices by JAX's collectives and lax.ppermute only.
A program may use at most 448 MiB of HBM per device.

v0:
```python
import functools
import math

import jax
import jax.numpy as jnp
from jax import lax
from jax.experimental import pallas as pl
from jax.experimental.pallas import tpu as pltpu
from jax.sharding import PartitionSpec as P

GSIZE = 16
VMEM = 56 * 1024 * 1024


def from_behind(value, axis, steps):
    count = lax.axis_size(axis)
    first, last = (max(0, -steps), min(count, count - steps))
    return lax.ppermute(value, axis, [(source, source + steps) for source in range(first, last)])


def params(*semantics):
    return pltpu.CompilerParams(dimension_semantics=semantics, vmem_limit_bytes=VMEM)


def filtered_rows(shifted, rows, rim, taps):
    count, reach = rows.shape[0], rim.shape[0]
    rows = rows.astype(jnp.float32)
    shifted[8 : 8 + count] = rows
    shifted[8 - reach : 8] = rim.astype(jnp.float32)
    total = taps[0:1] * rows
    for offset in range(1, reach + 1):
        total = total + taps[offset : offset + 1] * shifted[8 - offset : 8 - offset + count]
    return total


def product_kernel(place_ref, key_ref, value_ref, key_rim, value_rim, key_taps, value_taps, *refs, seq, outs):
    shifted, outs = refs[-1], refs[-1 - outs : -1]
    count, width = key_ref.shape[0], outs[0].shape[-1]
    spans, lane = key_ref.shape[-1] // (seq * width), shifted.shape[-1]
    for n in range(count):
        for span in range(spans):
            for part in range(seq):
                for low in range(0, width, lane):
                    start = (span * seq + part) * width + low
                    if len(outs) > 1 and lane % 128 == 0:
                        start = pl.multiple_of((span * seq + (place_ref[0] ^ part)) * width + low, lane)
                    lanes = pl.ds(start, lane)
                    keys = filtered_rows(
                        shifted.at[0], key_ref[n, 0, :, lanes], key_rim[n, 0, :, lanes], key_taps[0, :, lanes]
                    )
                    values = filtered_rows(
                        shifted.at[1], value_ref[n, 0, :, lanes], value_rim[n, 0, :, lanes], value_taps[0, :, lanes]
                    )
                    product = (keys * values).astype(jnp.bfloat16)
                    if len(outs) == 1:
                        outs[0][span, place_ref[0] ^ part, n, :, low : low + lane] = product
                    elif lane % 128 == 0:
                        outs[part][span, n, :, low : low + lane] = product
                    else:
                        for step in range(seq):

                            @pl.when((place_ref[0] ^ part) == step)
                            def _(step=step, n=n, span=span, low=low, product=product):
                                outs[step][span, n, :, low : low + lane] = product


def products(place, proj, rim, taps, first, count, seq, ch, joined, after=()):
    rows, channels = proj.shape[2:]
    width = channels // (ch * seq)
    spans = math.gcd(ch, 2)
    block, start = spans * seq * width, first // count

    def of(component, depth):
        return pl.BlockSpec((count, 1, depth, block), lambda j, *_: (start, component, 0, j))

    def tap_of(component):
        return pl.BlockSpec((1, taps.shape[1], block), lambda j, *_: (component, 0, j))

    if joined:
        out_specs = [pl.BlockSpec((spans, seq, count, rows, width), lambda j, *_: (j, 0, 0, 0, 0))]
        out_shape = [jax.ShapeDtypeStruct((ch, seq, count, rows, width), jnp.bfloat16)]
    else:
        out_specs = [pl.BlockSpec((spans, count, rows, width), lambda j, *_: (j, 0, 0, 0))] * seq
        out_shape = [jax.ShapeDtypeStruct((ch, count, rows, width), jnp.bfloat16)] * seq
    return pl.pallas_call(
        functools.partial(product_kernel, seq=seq, outs=len(out_shape)),
        grid_spec=pltpu.PrefetchScalarGridSpec(
            num_scalar_prefetch=1,
            grid=(ch // spans,),
            in_specs=[of(1, rows), of(2, rows), of(1, rim.shape[2]), of(2, rim.shape[2]), tap_of(1), tap_of(2)]
            + [pl.BlockSpec(memory_space=pl.ANY)] * len(after),
            out_specs=out_specs,
            scratch_shapes=[pltpu.VMEM((2, rows + 8, math.gcd(width, 128)), jnp.float32)],
        ),
        out_shape=out_shape,
        compiler_params=params("arbitrary"),
        cost_estimate=pl.CostEstimate(
            flops=20 * count * rows * channels, bytes_accessed=6 * count * rows * channels, transcendentals=0
        ),
        name="products",
    )(place, proj, proj, rim, rim, taps, taps, *after)


def queries_kernel(query_ref, query_rim, query_taps, out_ref, shifted):
    lane = shifted.shape[-1]
    for n in range(query_ref.shape[0]):
        for low in range(0, query_ref.shape[-1], lane):
            lanes = slice(low, low + lane)
            total = filtered_rows(shifted, query_ref[n, 0, :, lanes], query_rim[n, 0, :, lanes], query_taps[0, :, lanes])
            out_ref[n, :, lanes] = total.astype(jnp.bfloat16)


def short_queries(proj, rim, taps, ch):
    count, _, rows, channels = proj.shape
    block = channels // ch * math.gcd(ch, 2)

    def of(depth):
        return pl.BlockSpec((count, 1, depth, block), lambda j: (0, 0, 0, j))

    return pl.pallas_call(
        queries_kernel,
        grid=(channels // block,),
        in_specs=[of(rows), of(rim.shape[2]), pl.BlockSpec((1, taps.shape[1], block), lambda j: (0, 0, j))],
        out_specs=pl.BlockSpec((count, rows, block), lambda j: (0, 0, j)),
        out_shape=jax.ShapeDtypeStruct((count, rows, channels), jnp.bfloat16),
        scratch_shapes=[pltpu.VMEM((rows + 8, math.gcd(block, 128)), jnp.float32)],
        compiler_params=params("arbitrary"),
        cost_estimate=pl.CostEstimate(
            flops=8 * count * rows * channels, bytes_accessed=4 * count * rows * channels, transcendentals=0
        ),
        name="queries",
    )(proj, rim, taps)


def build_table(filter_row, table_ref):
    tile, length = table_ref.shape
    skewed = pltpu.roll(jnp.broadcast_to(filter_row, (tile, length)), 0, 1, stride=1, stride_axis=0)
    source = lax.broadcasted_iota(jnp.int32, (tile, tile), 0)
    target = lax.broadcasted_iota(jnp.int32, (tile, tile), 1)
    table_ref[:, :tile] = jnp.where(target >= source, skewed[:, :tile], 0.0).astype(jnp.bfloat16)
    if length > tile:
        table_ref[:, tile:] = skewed[:, tile:].astype(jnp.bfloat16)


def convolve(filter_ref, turned, table, acc, done, count):
    tile, length = table.shape[1:]
    tiles, strip = length // tile, count * GSIZE
    for group in range(table.shape[0]):
        build_table(filter_ref[group], table.at[group])
    for group in range(table.shape[0]):
        own = slice(group * GSIZE, (group + 1) * GSIZE)
        mine = turned[:, own, :].reshape(tiles * strip, tile)
        for lag in range(tiles):
            part = jnp.dot(
                mine[: (tiles - lag) * strip],
                table[group, :, lag * tile : (lag + 1) * tile],
                preferred_element_type=jnp.float32,
            )
            if lag == 0:
                acc[group] = part
            else:
                acc[group, lag * strip :] += part
        done[:, own, :] = acc[group].astype(jnp.bfloat16).reshape(tiles * count, GSIZE, tile)


def pieces_of(tile_index, span, ch):
    first, last, found = tile_index * span, (tile_index + 1) * span, []
    while first < last:
        stop = min(last, (first // ch + 1) * ch)
        found.append((first // ch, first % ch, first % ch + stop - first))
        first = stop
    return found


def conv_kernel(place_ref, *refs, seq, joined):
    turned, table, acc, done, gathered = refs[-5:]
    ch, _, count, rows, width = gathered.shape
    outs = refs[-5 - seq : -5] if joined else refs[-6:-5]
    ins, filter_ref = (refs[:1], refs[1]) if joined else (refs[:seq], refs[seq])
    tile, length = table.shape[1:]
    tiles, span = length // tile, tile // rows
    if joined:
        source = ins[0]
    else:
        source = gathered
        for step in range(seq):
            gathered[:, step] = ins[step][...]
    for u in range(tiles):
        for n in range(count):
            blocks = [
                source[low:high, place_ref[0] ^ z, n].reshape((high - low) * rows, width)
                for z, low, high in pieces_of(u, span, ch)
            ]
            block = blocks[0] if len(blocks) == 1 else jnp.concatenate(blocks, axis=0)
            turned[u * count + n] = block.T
    convolve(filter_ref, turned, table, acc, done, count)
    target = gathered if joined else outs[0]
    for u in range(tiles):
        for n in range(count):
            block, start = done[u * count + n].T, 0
            for z, low, high in pieces_of(u, span, ch):
                stop = start + (high - low) * rows
                target[low:high, place_ref[0] ^ z, n] = block[start:stop].reshape(high - low, rows, width)
                start = stop
    if joined:
        for step in range(seq):
            outs[step][...] = gathered[:, step]


def conv_scratch(count, width, tile, length):
    tiles, groups = length // tile, width // GSIZE
    return [
        pltpu.VMEM((tiles * count, width, tile), jnp.bfloat16),
        pltpu.VMEM((groups, tile, length), jnp.bfloat16),
        pltpu.VMEM((groups, tiles * count * GSIZE, tile), jnp.float32),
        pltpu.VMEM((tiles * count, width, tile), jnp.bfloat16),
    ]


def long_conv(place, pieces, filters, seq, after=()):
    joined = len(pieces) == 1
    ch, (count, rows, channels) = pieces[0].shape[0], pieces[0].shape[-3:]
    groups, _, length = filters.shape
    width, tile = math.gcd(channels, 128), min(256, length)
    tiles = length // tile
    one = pl.BlockSpec((ch, seq, count, rows, width), lambda j, place: (0, 0, 0, 0, j))
    part = pl.BlockSpec((ch, count, rows, width), lambda j, place: (0, 0, 0, j))
    whole_shape = jax.ShapeDtypeStruct((ch, seq, count, rows, channels), jnp.bfloat16)
    part_shape = jax.ShapeDtypeStruct((ch, count, rows, channels), jnp.bfloat16)
    return pl.pallas_call(
        functools.partial(conv_kernel, seq=seq, joined=joined),
        grid_spec=pltpu.PrefetchScalarGridSpec(
            num_scalar_prefetch=1,
            grid=(channels // width,),
            in_specs=([one] if joined else [part] * seq)
            + [pl.BlockSpec((width // GSIZE, 1, length), lambda j, place: (j, 0, 0))]
            + [pl.BlockSpec(memory_space=pl.ANY)] * len(after),
            out_specs=[part] * seq if joined else [one],
            scratch_shapes=conv_scratch(count, width, tile, length)
            + [pltpu.VMEM((ch, seq, count, rows, width), jnp.bfloat16)],
        ),
        out_shape=[part_shape] * seq if joined else [whole_shape],
        compiler_params=params("arbitrary"),
        cost_estimate=pl.CostEstimate(
            flops=groups * (tiles + 1) * tiles * tile * tile * count * GSIZE,
            bytes_accessed=4 * ch * seq * count * rows * channels,
            transcendentals=0,
        ),
        name="long_conv",
    )(place, *pieces, filters, *after)


def join_kernel(*refs, seq):
    for step in range(seq):
        refs[-1][:, step] = refs[step][...]


def join(pieces, after=()):
    seq, (ch, count, rows, width) = len(pieces), pieces[0].shape
    spans = math.gcd(ch, 4)
    return pl.pallas_call(
        functools.partial(join_kernel, seq=seq),
        grid=(ch // spans,),
        in_specs=[pl.BlockSpec((spans, count, rows, width), lambda j: (j, 0, 0, 0))] * seq
        + [pl.BlockSpec(memory_space=pl.ANY)] * len(after),
        out_specs=pl.BlockSpec((spans, seq, count, rows, width), lambda j: (j, 0, 0, 0, 0)),
        out_shape=jax.ShapeDtypeStruct((ch, seq, count, rows, width), jnp.bfloat16),
        compiler_params=params("arbitrary"),
        cost_estimate=pl.CostEstimate(flops=0, bytes_accessed=4 * seq * pieces[0].size, transcendentals=0),
        name="join",
    )(*pieces, *after)


def split_kernel(whole_ref, *refs, seq):
    for step in range(seq):
        refs[step - seq][...] = whole_ref[:, step]


def split(whole, after=()):
    ch, seq, count, rows, width = whole.shape
    spans = math.gcd(ch, 4)
    return pl.pallas_call(
        functools.partial(split_kernel, seq=seq),
        grid=(ch // spans,),
        in_specs=[pl.BlockSpec((spans, seq, count, rows, width), lambda j: (j, 0, 0, 0, 0))]
        + [pl.BlockSpec(memory_space=pl.ANY)] * len(after),
        out_specs=[pl.BlockSpec((spans, count, rows, width), lambda j: (j, 0, 0, 0))] * seq,
        out_shape=[jax.ShapeDtypeStruct((ch, count, rows, width), jnp.bfloat16)] * seq,
        compiler_params=params("arbitrary"),
        cost_estimate=pl.CostEstimate(flops=0, bytes_accessed=4 * whole.size, transcendentals=0),
        name="split",
    )(whole, *after)


def gate_kernel(place_ref, query_ref, *refs, seq, joined):
    out_ref = refs[-1]
    rows, width = out_ref.shape[1], refs[0].shape[-1]
    for home in range(1 if joined else seq):

        def gated(home=home):
            for n in range(query_ref.shape[0]):
                for span in range(refs[0].shape[0]):
                    for part in range(seq):
                        start = (span * seq + part) * width
                        lanes = slice(start, start + width)
                        if joined:
                            filtered = refs[0][span, place_ref[0] ^ part, n]
                        else:
                            filtered = refs[home ^ part][span, n]
                        value = query_ref[n, :, lanes].astype(jnp.float32) * filtered.astype(jnp.float32)
                        out_ref[n, :, lanes] = value.astype(jnp.bfloat16)

        if joined:
            gated()
        else:
            pl.when(place_ref[0] == home)(gated)


def gate(place, queries, pieces, first, seq):
    joined = len(pieces) == 1
    ch, (count, rows, width) = pieces[0].shape[0], pieces[0].shape[-3:]
    spans, start = math.gcd(ch, 2), first // count
    spec = pl.BlockSpec((count, rows, spans * seq * width), lambda j, place: (start, 0, j))
    one = pl.BlockSpec((spans, seq, count, rows, width), lambda j, place: (j, 0, 0, 0, 0))
    part = pl.BlockSpec((spans, count, rows, width), lambda j, place: (j, 0, 0, 0))
    return pl.pallas_call(
        functools.partial(gate_kernel, seq=seq, joined=joined),
        grid_spec=pltpu.PrefetchScalarGridSpec(
            num_scalar_prefetch=1,
            grid=(ch // spans,),
            in_specs=[spec] + ([one] if joined else [part] * seq),
            out_specs=spec,
        ),
        out_shape=jax.ShapeDtypeStruct(queries.shape, jnp.bfloat16),
        input_output_aliases={1: 0},
        compiler_params=params("arbitrary"),
        cost_estimate=pl.CostEstimate(
            flops=count * rows * queries.shape[-1],
            bytes_accessed=6 * count * rows * queries.shape[-1],
            transcendentals=0,
        ),
        name="gate",
    )(place, queries, *pieces)


def swap(pieces):
    count = lax.axis_size("seq")
    return [
        lax.ppermute(piece, "seq", [(source, source ^ step) for source in range(count)]) if step else piece
        for step, piece in enumerate(pieces)
    ]


def spread(whole):
    return lax.all_to_all(whole, "ch", split_axis=0, concat_axis=0, tiled=True)


def staged(times, place, step, *arrays):
    def round_of(_, held):
        return held[0] + 1, *step(held[0], *held[1:])

    return lax.fori_loop(0, times, round_of, (place, *arrays))[1:]


def shards(proj, short_w, long_filter):
    seq, ch = lax.axis_size("seq"), lax.axis_size("ch")
    tap_count, (seq_count, rows) = short_w.shape[0], proj.shape[:2]
    length, groups = long_filter.shape[1], long_filter.shape[0] // seq
    half = seq_count // 2
    place = lax.axis_index("seq").astype(jnp.int32).reshape(1)
    once = jnp.minimum(lax.axis_index("seq") + 1, 1)
    rim = from_behind(proj[:, rows - (tap_count - 1) :], ("seq", "ch"), 1).transpose(0, 2, 1, 3)
    taps = lax.all_gather(short_w, "ch", axis=2, tiled=True).transpose(1, 0, 2)
    turned = proj.transpose(0, 2, 1, 3)
    own = lax.dynamic_slice_in_dim(long_filter, place[0] * groups, groups, 0)
    filters = own.astype(jnp.float32).reshape(groups, 1, length)

    first = products(place, turned, rim, taps, 0, half, seq, ch, False)
    begun = first[0]

    def second_out(place, *held):
        (second,) = products(place, turned, rim, taps, half, half, seq, ch, True, after=[begun])
        return split(spread(second))

    second = staged(once, place, second_out, *[jnp.zeros_like(begun)] * seq)
    second_sent = second[0]

    def first_turn(place, *first):
        return long_conv(place, [spread(join(first, after=[place, second_sent]))], filters, seq)

    first = staged(once, place, first_turn, *swap(first))
    first_sent = first[0]

    def second_turn(place, *second):
        (second,) = long_conv(place, second, filters, seq, after=[first_sent])
        return split(spread(second))

    second = staged(once, place, second_turn, *swap(second))
    second_back = second[0]
    queries = short_queries(turned, rim, taps, ch)

    def first_gate(place, queries, *first):
        return gate(place, queries, [spread(join(first, after=[place, second_back]))], 0, seq), *first

    out = staged(once, place, first_gate, queries, *swap(first))[0]
    return gate(place, out, swap(second), half, seq)


def solution(mesh):
    in_specs = (P(None, ("seq", "ch"), None, None), P(None, None, "ch"), P("ch", None))
    out_specs = P(None, ("seq", "ch"), None)
    return jax.shard_map(shards, mesh=mesh, in_specs=in_specs, out_specs=out_specs, check_vma=False)
```

profile of v0, /device:TPU:8, one launch (start us, length us, event | category | flops | bytes accessed | tf_op | source)
XLA Modules:
  0.0 214.6 jit_solution(17441698959881221268)
XLA Ops:
  4.6 12.1 %all_gather.3 = f32[3,3,8192]{2,0,1:T(4,128)S(1)} all-gather(f32[3,3,1024]{2,0,1:T(4,128)S(1)} %copy.6), channel_id=1, replica_groups=mesh['seq'=4,'ch'=8] {'ch'}, dimensions={2}, use_global_device_ids=true | all-gather | bytes 331776 | tf_op jit(solution)/shard_map/all_gather | solution.py:373
  16.8 6.4 %products.2 = (bf16[8,2,64,256]{3,2,1,0:T(8,128)(2,1)S(1)}, bf16[8,2,64,256]{3,2,1,0:T(8,128)(2,1)}, bf16[8,2,64,256]{3,2,1,0:T(8,128)(2,1)}, bf16[8,2,64,256]{3,2,1,0:T(8,128)(2,1)}) custom-call(s32[1]{0:T(128)} %bitcast.place_ref, bf16[4,3,64,8192]{3,2,1,0:T(8,128)(2,1)} %bitcast.4, bf16[4,3,64,8192]{3,2,1,0:T(8,128)(2,1)} %bitcast.5, ...), custom_call_target="tpu_custom_call" | custom-call | flops 20971520 | bytes 6291456 | tf_op jit(solution)/shard_map/products/pallas_call | solution.py:85
  23.6 2.6 %collective-permute-start.2 = (bf16[8,2,64,256]{3,2,1,0:T(8,128)(2,1)}, bf16[8,2,64,256]{3,2,1,0:T(8,128)(2,1)}, u32[]{:S(2)}, u32[]{:S(2)}) collective-permute-start(bf16[8,2,64,256]{3,2,1,0:T(8,128)(2,1)} %get-tuple-element.230), channel_id=1, source_target_pairs={{0,16},{8,24},{16,0},{24,8},{1,17},{9,25},{17,1},{25,9},{2,18},{10... | collective-permute-start | bytes 1572872 | tf_op jit(solution)/shard_map/ppermute | solution.py:349
  31.0 39.5 %while.66 = (s32[]{:T(128)}, s32[1]{0:T(128)}, bf16[8,2,64,256]{3,2,1,0:T(8,128)(2,1)}, bf16[8,2,64,256]{3,2,1,0:T(8,128)(2,1)}, bf16[8,2,64,256]{3,2,1,0:T(8,12...) while((s32[]{:T(128)}, s32[1]{0:T(128)}, ...), condition=%wide.region_1.0_spmd, body=%wide.region_0.0_spmd.sunk | while | flops 20971524 | bytes 25166020 | solution.py:362
  31.0 5.4 %products.3 = bf16[8,4,2,64,256]{4,3,2,1,0:T(8,128)(2,1)} custom-call(s32[1]{0:T(128)} %get-tuple-element.587.place_ref, bf16[4,3,64,8192]{3,2,1,0:T(8,128)(2,1)} %get-tuple-element.606.key_ref.value_ref, bf16[4,3,64,8192]{3,2,1,0:T(8,128)(2,1)} %get-tuple-element.606.key_ref.value_ref, bf16[4,3,2,8192]{3,2,1,0:T(2,128)(2,1)S(1)} %get-tuple-element.607.key_rim.value_rim, ...), custom_call_target="tpu_custom_call" | custom-call | flops 20971520 | bytes 6291456 | tf_op jit(solution)/shard_map/while/body/products/pallas_call | solution.py:85
  36.4 3.6 %all-to-all-start = ((bf16[8,4,2,64,256]{4,3,2,1,0:T(8,128)(2,1)}), bf16[8,4,2,64,256]{4,3,2,1,0:T(8,128)(2,1)S(1)}, u32[]{:S(2)}, u32[]{:S(2)}) async-start(bf16[8,4,2,64,256]{4,3,2,1,0:T(8,128)(2,1)} %products.3), calls=%async_computation | async-start | bytes 4194304 | tf_op jit(solution)/shard_map/while/body/all_to_all | solution.py:355
  40.0 26.6 %all-to-all-done.whole_ref = bf16[8,4,2,64,256]{4,3,2,1,0:T(8,128)(2,1)S(1)} async-done(((bf16[8,4,2,64,256]{4,3,2,1,0:T(8,128)(2,1)}), bf16[8,4,2,64,256]{4,3,2,1,0:T(8,128)(2,1)S(1)}, u32[]{:S(2)}, u32[]{:S(2)}) %all-to-all-start) | async-done | bytes 2097184 | tf_op jit(solution)/shard_map/while/body/all_to_all | solution.py:355
  67.9 2.6 %split.2 = (bf16[8,2,64,256]{3,2,1,0:T(8,128)(2,1)}, bf16[8,2,64,256]{3,2,1,0:T(8,128)(2,1)}, bf16[8,2,64,256]{3,2,1,0:T(8,128)(2,1)}, bf16[8,2,64,256]{3,2,1,0:T(8,128)(2,1)}) custom-call(bf16[8,4,2,64,256]{4,3,2,1,0:T(8,128)(2,1)} %copy-done), custom_call_target="tpu_custom_call" | custom-call | bytes 4194304 | tf_op jit(solution)/shard_map/while/body/split/pallas_call | solution.py:282
  74.6 41.1 %while.67 = (s32[]{:T(128)}, s32[1]{0:T(128)}, bf16[8,2,64,256]{3,2,1,0:T(8,128)(2,1)S(1)}, bf16[8,2,64,256]{3,2,1,0:T(8,128)(2,1)}, bf16[8,2,64,256]{3,2,1,0:T(...) while((s32[]{:T(128)}, s32[1]{0:T(128)}, ...), condition=%wide.region_3.0_spmd, body=%wide.region_2.0_spmd.sunk | while | flops 2415919104 | bytes 23068860 | solution.py:362
  77.2 3.6 %all-to-all-start.1 = ((bf16[8,4,2,64,256]{4,3,2,1,0:T(8,128)(2,1)}), bf16[8,4,2,64,256]{4,3,2,1,0:T(8,128)(2,1)S(1)}, u32[]{:S(2)}, u32[]{:S(2)}) async-start(bf16[8,4,2,64,256]{4,3,2,1,0:T(8,128)(2,1)} %join.2), calls=%async_computation.1 | async-start | bytes 4194304 | tf_op jit(solution)/shard_map/while/body/all_to_all | solution.py:355
  80.8 26.6 %all-to-all-done.1.refs_0_ = bf16[8,4,2,64,256]{4,3,2,1,0:T(8,128)(2,1)S(1)} async-done(((bf16[8,4,2,64,256]{4,3,2,1,0:T(8,128)(2,1)}), bf16[8,4,2,64,256]{4,3,2,1,0:T(8,128)(2,1)S(1)}, u32[]{:S(2)}, u32[]{:S(2)}) %all-to-all-start.1) | async-done | bytes 2097184 | tf_op jit(solution)/shard_map/while/body/all_to_all | solution.py:355
  108.7 7.1 %long_conv.2 = (bf16[8,2,64,256]{3,2,1,0:T(8,128)(2,1)S(1)}, bf16[8,2,64,256]{3,2,1,0:T(8,128)(2,1)}, bf16[8,2,64,256]{3,2,1,0:T(8,128)(2,1)}, bf16[8,2,64,256]{3,2,1,0:T(8,128)(2,1)}) custom-call(s32[1]{0:T(128)S(6)} %copy.33.refs_4_.place_ref, bf16[8,4,2,64,256]{4,3,2,1,0:T(8,128)(2,1)} %copy-done.5, f32[16,1,2048]{2,1,0:T(1,128)S(1)} %get-tuple-element.642.refs_1_), custom_call_target="tpu_custom_call" | custom-call | flops 2415919104 | bytes 4194304 | tf_op jit(solution)/shard_map/while/body/long_conv/pallas_call | solution.py:230
  120.2 41.2 %while.68 = (s32[]{:T(128)}, s32[1]{0:T(128)}, bf16[8,2,64,256]{3,2,1,0:T(8,128)(2,1)}, bf16[8,2,64,256]{3,2,1,0:T(8,128)(2,1)}, bf16[8,2,64,256]{3,2,1,0:T(8,12...) while((s32[]{:T(128)}, s32[1]{0:T(128)}, ...), condition=%wide.region_5.0_spmd, body=%wide.region_4.0_spmd.sunk | while | flops 2415919104 | bytes 23068852 | solution.py:362
  120.2 7.0 %long_conv.3 = bf16[8,4,2,64,256]{4,3,2,1,0:T(8,128)(2,1)} custom-call(s32[1]{0:T(128)} %get-tuple-element.657.place_ref, bf16[8,2,64,256]{3,2,1,0:T(8,128)(2,1)} %get-tuple-element.658.refs_0_, bf16[8,2,64,256]{3,2,1,0:T(8,128)(2,1)} %get-tuple-element.659.refs_1_, bf16[8,2,64,256]{3,2,1,0:T(8,128)(2,1)} %get-tuple-element.660.refs_2_, ...), custom_call_target="tpu_custom_call" | custom-call | flops 2415919104 | bytes 4194304 | tf_op jit(solution)/shard_map/while/body/long_conv/pallas_call | solution.py:230
  127.2 3.6 %all-to-all-start.2 = ((bf16[8,4,2,64,256]{4,3,2,1,0:T(8,128)(2,1)}), bf16[8,4,2,64,256]{4,3,2,1,0:T(8,128)(2,1)S(1)}, u32[]{:S(2)}, u32[]{:S(2)}) async-start(bf16[8,4,2,64,256]{4,3,2,1,0:T(8,128)(2,1)} %long_conv.3), calls=%async_computation.2 | async-start | bytes 4194304 | tf_op jit(solution)/shard_map/while/body/all_to_all | solution.py:355
  130.8 26.6 %all-to-all-done.2.whole_ref = bf16[8,4,2,64,256]{4,3,2,1,0:T(8,128)(2,1)S(1)} async-done(((bf16[8,4,2,64,256]{4,3,2,1,0:T(8,128)(2,1)}), bf16[8,4,2,64,256]{4,3,2,1,0:T(8,128)(2,1)S(1)}, u32[]{:S(2)}, u32[]{:S(2)}) %all-to-all-start.2) | async-done | bytes 2097184 | tf_op jit(solution)/shard_map/while/body/all_to_all | solution.py:355
  158.7 2.6 %split.3 = (bf16[8,2,64,256]{3,2,1,0:T(8,128)(2,1)}, bf16[8,2,64,256]{3,2,1,0:T(8,128)(2,1)}, bf16[8,2,64,256]{3,2,1,0:T(8,128)(2,1)}, bf16[8,2,64,256]{3,2,1,0:T(8,128)(2,1)}) custom-call(bf16[8,4,2,64,256]{4,3,2,1,0:T(8,128)(2,1)} %copy-done.1), custom_call_target="tpu_custom_call" | custom-call | bytes 4194304 | tf_op jit(solution)/shard_map/while/body/split/pallas_call | solution.py:282
  165.8 6.1 %queries.1 = bf16[4,64,8192]{2,1,0:T(8,128)(2,1)} custom-call(bf16[4,3,64,8192]{3,2,1,0:T(8,128)(2,1)} %get-tuple-element.711, bf16[4,3,2,8192]{3,2,1,0:T(2,128)(2,1)} %copy-done.4, f32[3,3,8192]{2,1,0:T(4,128)S(1)} %get-tuple-element.723), custom_call_target="tpu_custom_call" | custom-call | flops 16777216 | bytes 8388608 | tf_op jit(solution)/shard_map/queries/pallas_call | solution.py:120
  171.9 38.4 %while.69 = (s32[]{:T(128)}, s32[1]{0:T(128)}, bf16[4,64,8192]{2,1,0:T(8,128)(2,1)}, s32[]{:T(128)}, bf16[8,2,64,256]{3,2,1,0:T(8,128)(2,1)S(1)}, /*index=5*/bf1...) while((s32[]{:T(128)}, s32[1]{0:T(128)}, ...), condition=%wide.region_7.0_spmd, body=%wide.region_6.0_spmd.sunk | while | flops 1048579 | bytes 25166012 | solution.py:362
  171.9 2.5 %join.3 = bf16[8,4,2,64,256]{4,3,2,1,0:T(8,128)(2,1)} custom-call(bf16[8,2,64,256]{3,2,1,0:T(8,128)(2,1)S(1)} %get-tuple-element.704.refs_0_, bf16[8,2,64,256]{3,2,1,0:T(8,128)(2,1)} %get-tuple-element.705.refs_1_, bf16[8,2,64,256]{3,2,1,0:T(8,128)(2,1)} %get-tuple-element.706.refs_2_, bf16[8,2,64,256]{3,2,1,0:T(8,128)(2,1)} %get-tuple-element.707.refs_3_, ...), custom_call_target="tpu_custom_call" | custom-call | bytes 4194304 | tf_op jit(solution)/shard_map/while/body/join/pallas_call | solution.py:261
  174.5 3.6 %all-to-all-start.3 = ((bf16[8,4,2,64,256]{4,3,2,1,0:T(8,128)(2,1)}), bf16[8,4,2,64,256]{4,3,2,1,0:T(8,128)(2,1)S(1)}, u32[]{:S(2)}, u32[]{:S(2)}) async-start(bf16[8,4,2,64,256]{4,3,2,1,0:T(8,128)(2,1)} %join.3), calls=%async_computation.3 | async-start | bytes 4194304 | tf_op jit(solution)/shard_map/while/body/all_to_all | solution.py:355
  178.1 26.6 %all-to-all-done.3.refs_0_ = bf16[8,4,2,64,256]{4,3,2,1,0:T(8,128)(2,1)S(1)} async-done(((bf16[8,4,2,64,256]{4,3,2,1,0:T(8,128)(2,1)}), bf16[8,4,2,64,256]{4,3,2,1,0:T(8,128)(2,1)S(1)}, u32[]{:S(2)}, u32[]{:S(2)}) %all-to-all-start.3) | async-done | bytes 2097184 | tf_op jit(solution)/shard_map/while/body/all_to_all | solution.py:355
  206.0 4.3 %gate.3 = bf16[4,64,8192]{2,1,0:T(8,128)(2,1)} custom-call(s32[1]{0:T(128)S(6)} %copy.66.refs_4_.place_ref, bf16[4,64,8192]{2,1,0:T(8,128)(2,1)} %get-tuple-element.691.query_ref, bf16[8,4,2,64,256]{4,3,2,1,0:T(8,128)(2,1)} %copy-done.2), custom_call_target="tpu_custom_call", output_to_operand_aliasing={{}: (1, {})} | custom-call | flops 1048576 | bytes 6291456 | tf_op jit(solution)/shard_map/while/body/gate/pallas_call | solution.py:326
  210.4 4.3 %gate.2 = bf16[4,64,8192]{2,1,0:T(8,128)(2,1)} custom-call(s32[1]{0:T(128)} %bitcast.place_ref, bf16[4,64,8192]{2,1,0:T(8,128)(2,1)} %get-tuple-element.241.query_ref, bf16[8,2,64,256]{3,2,1,0:T(8,128)(2,1)S(1)} %get-tuple-element.725, bf16[8,2,64,256]{3,2,1,0:T(8,128)(2,1)} %collective-permute-done.10.refs_1_, ...), custom_call_target="tpu_custom_call", output_to_operand_aliasing={{}: (1, {})} | custom-call | flops 1048576 | bytes 6291456 | tf_op jit(solution)/shard_map/gate/pallas_call | solution.py:326
  (46 shorter events, 30.5 us)
Async XLA Ops:
  1.9 14.9 %collective-permute-start = (bf16[4,2,3,8192]{3,1,2,0:T(2,128)(2,1)S(1)}, bf16[4,2,3,8192]{3,1,2,0:T(2,128)(2,1)S(1)}, u32[]{:S(2)}, u32[]{:S(2)}) collective-permute-start(bf16[4,2,3,8192]{3,1,2,0:T(2,128)(2,1)S(1)} %slice.3), channel_id=1, source_target_pairs={{0,1},{1,2},{2,3},{3,4},{4,5},{5,6},{6,7},{7,8},{8,9},{9,10},{10,1... | collective-permute-start | bytes 1179656 | tf_op jit(solution)/shard_map/ppermute | solution.py:18
  23.2 51.0 %collective-permute-start.1 = (bf16[8,2,64,256]{3,2,1,0:T(8,128)(2,1)}, bf16[8,2,64,256]{3,2,1,0:T(8,128)(2,1)}, u32[]{:S(2)}, u32[]{:S(2)}) collective-permute-start(bf16[8,2,64,256]{3,2,1,0:T(8,128)(2,1)} %get-tuple-element.229), channel_id=1, source_target_pairs={{0,8},{8,0},{16,24},{24,16},{1,9},{9,1},{17,25},{25,17},{2,10},{10... | collective-permute-start | bytes 1572872 | tf_op jit(solution)/shard_map/ppermute | solution.py:349
  23.6 51.0 %collective-permute-start.2 = (bf16[8,2,64,256]{3,2,1,0:T(8,128)(2,1)}, bf16[8,2,64,256]{3,2,1,0:T(8,128)(2,1)}, u32[]{:S(2)}, u32[]{:S(2)}) collective-permute-start(bf16[8,2,64,256]{3,2,1,0:T(8,128)(2,1)} %get-tuple-element.230), channel_id=1, source_target_pairs={{0,16},{8,24},{16,0},{24,8},{1,17},{9,25},{17,1},{25,9},{2,18},{10... | collective-permute-start | bytes 1572872 | tf_op jit(solution)/shard_map/ppermute | solution.py:349
  26.2 48.4 %collective-permute-start.3 = (bf16[8,2,64,256]{3,2,1,0:T(8,128)(2,1)}, bf16[8,2,64,256]{3,2,1,0:T(8,128)(2,1)}, u32[]{:S(2)}, u32[]{:S(2)}) collective-permute-start(bf16[8,2,64,256]{3,2,1,0:T(8,128)(2,1)} %get-tuple-element.231), channel_id=1, source_target_pairs={{0,24},{8,16},{16,8},{24,0},{1,25},{9,17},{17,9},{25,1},{2,26},{10... | collective-permute-start | bytes 1572872 | tf_op jit(solution)/shard_map/ppermute | solution.py:349
  36.4 30.2 %all-to-all-start = ((bf16[8,4,2,64,256]{4,3,2,1,0:T(8,128)(2,1)}), bf16[8,4,2,64,256]{4,3,2,1,0:T(8,128)(2,1)S(1)}, u32[]{:S(2)}, u32[]{:S(2)}) async-start(bf16[8,4,2,64,256]{4,3,2,1,0:T(8,128)(2,1)} %products.3), calls=%async_computation | async-start | bytes 4194304 | tf_op jit(solution)/shard_map/while/body/all_to_all | solution.py:355
  66.6 1.3 copy-start
  70.6 4.1 %copy-start.4 = (bf16[4,3,2,8192]{3,2,1,0:T(2,128)(2,1)}, bf16[4,3,2,8192]{3,2,1,0:T(2,128)(2,1)S(1)}, u32[]{:S(2)}) copy-start(bf16[4,3,2,8192]{3,2,1,0:T(2,128)(2,1)S(1)} %get-tuple-element.727) | copy-start | bytes 1179652
  70.6 49.0 %collective-permute-start.7 = (bf16[8,2,64,256]{3,2,1,0:T(8,128)(2,1)}, bf16[8,2,64,256]{3,2,1,0:T(8,128)(2,1)}, u32[]{:S(2)}, u32[]{:S(2)}) collective-permute-start(bf16[8,2,64,256]{3,2,1,0:T(8,128)(2,1)} %get-tuple-element.237), channel_id=1, source_target_pairs={{0,8},{8,0},{16,24},{24,16},{1,9},{9,1},{17,25},{25,17},{2,10},{10... | collective-permute-start | bytes 1572872 | tf_op jit(solution)/shard_map/ppermute | solution.py:349
  71.9 48.3 %collective-permute-start.8 = (bf16[8,2,64,256]{3,2,1,0:T(8,128)(2,1)}, bf16[8,2,64,256]{3,2,1,0:T(8,128)(2,1)}, u32[]{:S(2)}, u32[]{:S(2)}) collective-permute-start(bf16[8,2,64,256]{3,2,1,0:T(8,128)(2,1)} %get-tuple-element.238), channel_id=1, source_target_pairs={{0,16},{8,24},{16,0},{24,8},{1,17},{9,25},{17,1},{25,9},{2,18},{10... | collective-permute-start | bytes 1572872 | tf_op jit(solution)/shard_map/ppermute | solution.py:349
  74.1 46.0 %collective-permute-start.9 = (bf16[8,2,64,256]{3,2,1,0:T(8,128)(2,1)}, bf16[8,2,64,256]{3,2,1,0:T(8,128)(2,1)}, u32[]{:S(2)}, u32[]{:S(2)}) collective-permute-start(bf16[8,2,64,256]{3,2,1,0:T(8,128)(2,1)} %get-tuple-element.239), channel_id=1, source_target_pairs={{0,24},{8,16},{16,8},{24,0},{1,25},{9,17},{17,9},{25,1},{2,26},{10... | collective-permute-start | bytes 1572872 | tf_op jit(solution)/shard_map/ppermute | solution.py:349
  77.2 30.2 %all-to-all-start.1 = ((bf16[8,4,2,64,256]{4,3,2,1,0:T(8,128)(2,1)}), bf16[8,4,2,64,256]{4,3,2,1,0:T(8,128)(2,1)S(1)}, u32[]{:S(2)}, u32[]{:S(2)}) async-start(bf16[8,4,2,64,256]{4,3,2,1,0:T(8,128)(2,1)} %join.2), calls=%async_computation.1 | async-start | bytes 4194304 | tf_op jit(solution)/shard_map/while/body/all_to_all | solution.py:355
  107.3 1.3 copy-start.5
  115.8 49.5 %collective-permute-start.4 = (bf16[8,2,64,256]{3,2,1,0:T(8,128)(2,1)}, bf16[8,2,64,256]{3,2,1,0:T(8,128)(2,1)}, u32[]{:S(2)}, u32[]{:S(2)}) collective-permute-start(bf16[8,2,64,256]{3,2,1,0:T(8,128)(2,1)} %get-tuple-element.234), channel_id=1, source_target_pairs={{0,8},{8,0},{16,24},{24,16},{1,9},{9,1},{17,25},{25,17},{2,10},{10... | collective-permute-start | bytes 1572872 | tf_op jit(solution)/shard_map/ppermute | solution.py:349
  117.5 54.4 %collective-permute-start.5 = (bf16[8,2,64,256]{3,2,1,0:T(8,128)(2,1)}, bf16[8,2,64,256]{3,2,1,0:T(8,128)(2,1)}, u32[]{:S(2)}, u32[]{:S(2)}) collective-permute-start(bf16[8,2,64,256]{3,2,1,0:T(8,128)(2,1)} %get-tuple-element.235), channel_id=1, source_target_pairs={{0,16},{8,24},{16,0},{24,8},{1,17},{9,25},{17,1},{25,9},{2,18},{10... | collective-permute-start | bytes 1572872 | tf_op jit(solution)/shard_map/ppermute | solution.py:349
  119.6 52.3 %collective-permute-start.6 = (bf16[8,2,64,256]{3,2,1,0:T(8,128)(2,1)}, bf16[8,2,64,256]{3,2,1,0:T(8,128)(2,1)}, u32[]{:S(2)}, u32[]{:S(2)}) collective-permute-start(bf16[8,2,64,256]{3,2,1,0:T(8,128)(2,1)} %get-tuple-element.236), channel_id=1, source_target_pairs={{0,24},{8,16},{16,8},{24,0},{1,25},{9,17},{17,9},{25,1},{2,26},{10... | collective-permute-start | bytes 1572872 | tf_op jit(solution)/shard_map/ppermute | solution.py:349
  127.2 30.2 %all-to-all-start.2 = ((bf16[8,4,2,64,256]{4,3,2,1,0:T(8,128)(2,1)}), bf16[8,4,2,64,256]{4,3,2,1,0:T(8,128)(2,1)S(1)}, u32[]{:S(2)}, u32[]{:S(2)}) async-start(bf16[8,4,2,64,256]{4,3,2,1,0:T(8,128)(2,1)} %long_conv.3), calls=%async_computation.2 | async-start | bytes 4194304 | tf_op jit(solution)/shard_map/while/body/all_to_all | solution.py:355
  157.4 1.3 copy-start.1
  161.4 49.0 %collective-permute-start.10 = (bf16[8,2,64,256]{3,2,1,0:T(8,128)(2,1)}, bf16[8,2,64,256]{3,2,1,0:T(8,128)(2,1)}, u32[]{:S(2)}, u32[]{:S(2)}) collective-permute-start(bf16[8,2,64,256]{3,2,1,0:T(8,128)(2,1)} %get-tuple-element.242), channel_id=1, source_target_pairs={{0,8},{8,0},{16,24},{24,16},{1,9},{9,1},{17,25},{25,17},{2,10},{10... | collective-permute-start | bytes 1572872 | tf_op jit(solution)/shard_map/ppermute | solution.py:349
  163.1 47.3 %collective-permute-start.11 = (bf16[8,2,64,256]{3,2,1,0:T(8,128)(2,1)}, bf16[8,2,64,256]{3,2,1,0:T(8,128)(2,1)}, u32[]{:S(2)}, u32[]{:S(2)}) collective-permute-start(bf16[8,2,64,256]{3,2,1,0:T(8,128)(2,1)} %get-tuple-element.243), channel_id=1, source_target_pairs={{0,16},{8,24},{16,0},{24,8},{1,17},{9,25},{17,1},{25,9},{2,18},{10... | collective-permute-start | bytes 1572872 | tf_op jit(solution)/shard_map/ppermute | solution.py:349
  165.2 45.1 %collective-permute-start.12 = (bf16[8,2,64,256]{3,2,1,0:T(8,128)(2,1)}, bf16[8,2,64,256]{3,2,1,0:T(8,128)(2,1)}, u32[]{:S(2)}, u32[]{:S(2)}) collective-permute-start(bf16[8,2,64,256]{3,2,1,0:T(8,128)(2,1)} %get-tuple-element.244), channel_id=1, source_target_pairs={{0,24},{8,16},{16,8},{24,0},{1,25},{9,17},{17,9},{25,1},{2,26},{10... | collective-permute-start | bytes 1572872 | tf_op jit(solution)/shard_map/ppermute | solution.py:349
  165.8 6.1 %copy-start.3 = (bf16[8,2,64,256]{3,2,1,0:T(8,128)(2,1)S(1)}, bf16[8,2,64,256]{3,2,1,0:T(8,128)(2,1)}, u32[]{:S(2)}) copy-start(bf16[8,2,64,256]{3,2,1,0:T(8,128)(2,1)} %get-tuple-element.686.refs_0_) | copy-start | bytes 1572868
  174.5 30.2 %all-to-all-start.3 = ((bf16[8,4,2,64,256]{4,3,2,1,0:T(8,128)(2,1)}), bf16[8,4,2,64,256]{4,3,2,1,0:T(8,128)(2,1)S(1)}, u32[]{:S(2)}, u32[]{:S(2)}) async-start(bf16[8,4,2,64,256]{4,3,2,1,0:T(8,128)(2,1)} %join.3), calls=%async_computation.3 | async-start | bytes 4194304 | tf_op jit(solution)/shard_map/while/body/all_to_all | solution.py:355
  204.7 1.4 copy-start.2
where the time goes:
time: 218 us; the launch traced here: 215 us
  waiting for transfers between devices  106 us (49%)
  Pallas kernels  51 us (23%)
  starting transfers between devices  32.7 us (15%)
  blocking collectives  12.1 us (6%)
  local copies, waits for them, and re-layouts  11.5 us (5%)
    all_to_all x4, waiting for transfers between devices, spread(): return lax.all_to_all(whole, 'ch', split_axis=0, concat_axis=0, tiled=True)  106 us
    ppermute x12, starting transfers between devices, swap(): lax.ppermute(piece, 'seq', [(source, source ^ step) for source in range(c...  16.3 us
    all_to_all x4, starting transfers between devices, spread(): return lax.all_to_all(whole, 'ch', split_axis=0, concat_axis=0, tiled=True)  14.4 us
    pallas_call x2, Pallas kernels, long_conv(): pl.pallas_call(functools.partial(conv_kernel, seq=seq, joined=joined), gr...  14.2 us
    all_gather x1, blocking collectives, shards(): taps = lax.all_gather(short_w, 'ch', axis=2, tiled=True).transpose(1, 0, 2)  12.1 us
    pallas_call x2, Pallas kernels, products(): pl.pallas_call(functools.partial(product_kernel, seq=seq, outs=len(out_sh...  11.8 us
    pallas_call x2, Pallas kernels, gate(): pl.pallas_call(functools.partial(gate_kernel, seq=seq, joined=joined), gr...  8.57 us
    pallas_call x1, Pallas kernels, short_queries(): pl.pallas_call(queries_kernel, grid=(channels // block,), in_specs=[of(ro...  6.13 us
  transfers between devices with their start and end apart: 17, of which 4 were waited for; matrix products, arithmetic and copies ran while one was open for 2% of the time, Pallas kernels for 19%

commit v1 on v0

--- a/solution.py
+++ b/solution.py
@@ -9,7 +9,7 @@
 from jax.sharding import PartitionSpec as P
 
 GSIZE = 16
-VMEM = 56 * 1024 * 1024
+MIB = 1024 * 1024
 
 
 def from_behind(value, axis, steps):
@@ -18,8 +18,8 @@
     return lax.ppermute(value, axis, [(source, source + steps) for source in range(first, last)])
 
 
-def params(*semantics):
-    return pltpu.CompilerParams(dimension_semantics=semantics, vmem_limit_bytes=VMEM)
+def params(mib, *semantics):
+    return pltpu.CompilerParams(dimension_semantics=semantics, vmem_limit_bytes=mib * MIB)
 
 
 def filtered_rows(shifted, rows, rim, taps):
@@ -33,7 +33,7 @@
     return total
 
 
-def product_kernel(place_ref, key_ref, value_ref, key_rim, value_rim, key_taps, value_taps, *refs, seq, outs):
+def product_kernel(place_ref, key_ref, value_ref, key_rim, value_rim, taps_ref, *refs, seq, outs):
     shifted, outs = refs[-1], refs[-1 - outs : -1]
     count, width = key_ref.shape[0], outs[0].shape[-1]
     spans, lane = key_ref.shape[-1] // (seq * width), shifted.shape[-1]
@@ -46,10 +46,10 @@
                         start = pl.multiple_of((span * seq + (place_ref[0] ^ part)) * width + low, lane)
                     lanes = pl.ds(start, lane)
                     keys = filtered_rows(
-                        shifted.at[0], key_ref[n, 0, :, lanes], key_rim[n, 0, :, lanes], key_taps[0, :, lanes]
+                        shifted.at[0], key_ref[n, 0, :, lanes], key_rim[n, 0, :, lanes], taps_ref[:, 1, lanes]
                     )
                     values = filtered_rows(
-                        shifted.at[1], value_ref[n, 0, :, lanes], value_rim[n, 0, :, lanes], value_taps[0, :, lanes]
+                        shifted.at[1], value_ref[n, 0, :, lanes], value_rim[n, 0, :, lanes], taps_ref[:, 2, lanes]
                     )
                     product = (keys * values).astype(jnp.bfloat16)
                     if len(outs) == 1:
@@ -73,9 +73,6 @@
     def of(component, depth):
         return pl.BlockSpec((count, 1, depth, block), lambda j, *_: (start, component, 0, j))
 
-    def tap_of(component):
-        return pl.BlockSpec((1, taps.shape[1], block), lambda j, *_: (component, 0, j))
-
     if joined:
         out_specs = [pl.BlockSpec((spans, seq, count, rows, width), lambda j, *_: (j, 0, 0, 0, 0))]
         out_shape = [jax.ShapeDtypeStruct((ch, seq, count, rows, width), jnp.bfloat16)]
@@ -87,30 +84,32 @@
         grid_spec=pltpu.PrefetchScalarGridSpec(
             num_scalar_prefetch=1,
             grid=(ch // spans,),
-            in_specs=[of(1, rows), of(2, rows), of(1, rim.shape[2]), of(2, rim.shape[2]), tap_of(1), tap_of(2)]
+            in_specs=[of(1, rows), of(2, rows), of(1, rim.shape[2]), of(2, rim.shape[2])]
+            + [pl.BlockSpec(taps.shape[:2] + (block,), lambda j, *_: (0, 0, j))]
             + [pl.BlockSpec(memory_space=pl.ANY)] * len(after),
             out_specs=out_specs,
             scratch_shapes=[pltpu.VMEM((2, rows + 8, math.gcd(width, 128)), jnp.float32)],
         ),
         out_shape=out_shape,
-        compiler_params=params("arbitrary"),
+        compiler_params=params(8, "arbitrary"),
         cost_estimate=pl.CostEstimate(
             flops=20 * count * rows * channels, bytes_accessed=6 * count * rows * channels, transcendentals=0
         ),
         name="products",
-    )(place, proj, proj, rim, rim, taps, taps, *after)
-
-
-def queries_kernel(query_ref, query_rim, query_taps, out_ref, shifted):
+    )(place, proj, proj, rim, rim, taps, *after)
+
+
+def queries_kernel(query_ref, query_rim, query_taps, *refs):
+    out_ref, shifted = refs[-2:]
     lane = shifted.shape[-1]
     for n in range(query_ref.shape[0]):
         for low in range(0, query_ref.shape[-1], lane):
             lanes = slice(low, low + lane)
-            total = filtered_rows(shifted, query_ref[n, 0, :, lanes], query_rim[n, 0, :, lanes], query_taps[0, :, lanes])
+            total = filtered_rows(shifted, query_ref[n, 0, :, lanes], query_rim[n, 0, :, lanes], query_taps[:, 0, lanes])
             out_ref[n, :, lanes] = total.astype(jnp.bfloat16)
 
 
-def short_queries(proj, rim, taps, ch):
+def short_queries(proj, rim, taps, ch, after=()):
     count, _, rows, channels = proj.shape
     block = channels // ch * math.gcd(ch, 2)
 
@@ -120,16 +119,17 @@
     return pl.pallas_call(
         queries_kernel,
         grid=(channels // block,),
-        in_specs=[of(rows), of(rim.shape[2]), pl.BlockSpec((1, taps.shape[1], block), lambda j: (0, 0, j))],
+        in_specs=[of(rows), of(rim.shape[2]), pl.BlockSpec(taps.shape[:2] + (block,), lambda j: (0, 0, j))]
+        + [pl.BlockSpec(memory_space=pl.ANY)] * len(after),
         out_specs=pl.BlockSpec((count, rows, block), lambda j: (0, 0, j)),
         out_shape=jax.ShapeDtypeStruct((count, rows, channels), jnp.bfloat16),
         scratch_shapes=[pltpu.VMEM((rows + 8, math.gcd(block, 128)), jnp.float32)],
-        compiler_params=params("arbitrary"),
+        compiler_params=params(8, "arbitrary"),
         cost_estimate=pl.CostEstimate(
             flops=8 * count * rows * channels, bytes_accessed=4 * count * rows * channels, transcendentals=0
         ),
         name="queries",
-    )(proj, rim, taps)
+    )(proj, rim, taps, *after)
 
 
 def build_table(filter_row, table_ref):
@@ -240,7 +240,7 @@
             + [pltpu.VMEM((ch, seq, count, rows, width), jnp.bfloat16)],
         ),
         out_shape=[part_shape] * seq if joined else [whole_shape],
-        compiler_params=params("arbitrary"),
+        compiler_params=params(32, "arbitrary"),
         cost_estimate=pl.CostEstimate(
             flops=groups * (tiles + 1) * tiles * tile * tile * count * GSIZE,
             bytes_accessed=4 * ch * seq * count * rows * channels,
@@ -265,7 +265,7 @@
         + [pl.BlockSpec(memory_space=pl.ANY)] * len(after),
         out_specs=pl.BlockSpec((spans, seq, count, rows, width), lambda j: (j, 0, 0, 0, 0)),
         out_shape=jax.ShapeDtypeStruct((ch, seq, count, rows, width), jnp.bfloat16),
-        compiler_params=params("arbitrary"),
+        compiler_params=params(8, "arbitrary"),
         cost_estimate=pl.CostEstimate(flops=0, bytes_accessed=4 * seq * pieces[0].size, transcendentals=0),
         name="join",
     )(*pieces, *after)
@@ -286,7 +286,7 @@
         + [pl.BlockSpec(memory_space=pl.ANY)] * len(after),
         out_specs=[pl.BlockSpec((spans, count, rows, width), lambda j: (j, 0, 0, 0))] * seq,
         out_shape=[jax.ShapeDtypeStruct((ch, count, rows, width), jnp.bfloat16)] * seq,
-        compiler_params=params("arbitrary"),
+        compiler_params=params(8, "arbitrary"),
         cost_estimate=pl.CostEstimate(flops=0, bytes_accessed=4 * whole.size, transcendentals=0),
         name="split",
     )(whole, *after)
@@ -333,7 +333,7 @@
         ),
         out_shape=jax.ShapeDtypeStruct(queries.shape, jnp.bfloat16),
         input_output_aliases={1: 0},
-        compiler_params=params("arbitrary"),
+        compiler_params=params(8, "arbitrary"),
         cost_estimate=pl.CostEstimate(
             flops=count * rows * queries.shape[-1],
             bytes_accessed=6 * count * rows * queries.shape[-1],
@@ -353,6 +353,19 @@
 
 def spread(whole):
     return lax.all_to_all(whole, "ch", split_axis=0, concat_axis=0, tiled=True)
+
+
+def vacant_kernel(*refs):
+    pass
+
+
+def vacant(*arrays):
+    return pl.pallas_call(
+        vacant_kernel,
+        out_specs=[pl.BlockSpec(memory_space=pl.ANY)] * len(arrays),
+        out_shape=[jax.ShapeDtypeStruct(array.shape, array.dtype) for array in arrays],
+        name="vacant",
+    )()
 
 
 def staged(times, place, step, *arrays):
@@ -370,7 +383,7 @@
     place = lax.axis_index("seq").astype(jnp.int32).reshape(1)
     once = jnp.minimum(lax.axis_index("seq") + 1, 1)
     rim = from_behind(proj[:, rows - (tap_count - 1) :], ("seq", "ch"), 1).transpose(0, 2, 1, 3)
-    taps = lax.all_gather(short_w, "ch", axis=2, tiled=True).transpose(1, 0, 2)
+    taps = lax.all_gather(short_w, "ch", axis=2, tiled=True)
     turned = proj.transpose(0, 2, 1, 3)
     own = lax.dynamic_slice_in_dim(long_filter, place[0] * groups, groups, 0)
     filters = own.astype(jnp.float32).reshape(groups, 1, length)
@@ -379,10 +392,12 @@
     begun = first[0]
 
     def second_out(place, *held):
-        (second,) = products(place, turned, rim, taps, half, half, seq, ch, True, after=[begun])
-        return split(spread(second))
-
-    second = staged(once, place, second_out, *[jnp.zeros_like(begun)] * seq)
+        (second,) = products(place, turned, rim, taps, half, half, seq, ch, True, after=[begun, place])
+        queries = short_queries(turned, rim, taps, ch, after=[place])
+        return queries, *split(spread(second))
+
+    shape = jax.ShapeDtypeStruct((seq_count, rows, proj.shape[3]), proj.dtype)
+    queries, *second = staged(once, place, second_out, *vacant(shape, *first))
     second_sent = second[0]
 
     def first_turn(place, *first):
@@ -397,7 +412,6 @@
 
     second = staged(once, place, second_turn, *swap(second))
     second_back = second[0]
-    queries = short_queries(turned, rim, taps, ch)
 
     def first_gate(place, queries, *first):
         return gate(place, queries, [spread(join(first, after=[place, second_back]))], 0, seq), *first

time: 218 us -> 212 us (0.972); the launches traced: 215 us -> 211 us
  waiting for transfers between devices: 106 us -> 115 us
  local copies, waits for them, and re-layouts: 11.5 us -> 3.93 us
  Pallas kernels: 51 us -> 45.8 us
    ppermute x12, waiting for transfers between devices: 0.03 us -> 15.2 us  [swap(): lax.ppermute(piece, 'seq', [(source, source ^ step) for source in range(c...]
    all_to_all x4, waiting for transfers between devices: 106 us -> 100 us  [spread(): return lax.all_to_all(whole, 'ch', split_axis=0, concat_axis=0, tiled=True)]
    while x8 -> x4, local copies, waits for them, and re-layouts: 5.31 us -> 1.34 us
    broadcast_in_dim x4 -> x0, local copies, waits for them, and re-layouts: 3.4 us -> none  [shards(): second = staged(once, place, second_out, *[jnp.zeros_like(begun)] * seq)]
    pallas_call x2, Pallas kernels: 5.29 us -> 2.88 us  [split(): pl.pallas_call(functools.partial(split_kernel, seq=seq), grid=(ch // span...]
  transfers between devices with their start and end apart: 17 -> 17, of which waited for: 4 -> 8; matrix products, arithmetic and copies ran while one was open for 2% -> 1% of each run, Pallas kernels for 19% -> 17%
where the time goes in v1:
time: 212 us; the launch traced here: 211 us
  waiting for transfers between devices  115 us (54%)
  Pallas kernels  45.8 us (22%)
  starting transfers between devices  31.3 us (15%)
  blocking collectives  13.8 us (7%)
  local copies, waits for them, and re-layouts  3.93 us (2%)
    all_to_all x4, waiting for transfers between devices, spread(): return lax.all_to_all(whole, 'ch', split_axis=0, concat_axis=0, tiled=True)  100 us
    ppermute x12, waiting for transfers between devices, swap(): lax.ppermute(piece, 'seq', [(source, source ^ step) for source in range(c...  15.2 us
    ppermute x12, starting transfers between devices, swap(): lax.ppermute(piece, 'seq', [(source, source ^ step) for source in range(c...  15 us
    all_to_all x4, starting transfers between devices, spread(): return lax.all_to_all(whole, 'ch', split_axis=0, concat_axis=0, tiled=True)  14.4 us
    all_gather x1, blocking collectives, shards(): taps = lax.all_gather(short_w, 'ch', axis=2, tiled=True)  13.8 us
    pallas_call x2, Pallas kernels, long_conv(): pl.pallas_call(functools.partial(conv_kernel, seq=seq, joined=joined), gr...  12.7 us
    pallas_call x2, Pallas kernels, products(): pl.pallas_call(functools.partial(product_kernel, seq=seq, outs=len(out_sh...  10.7 us
    pallas_call x2, Pallas kernels, gate(): pl.pallas_call(functools.partial(gate_kernel, seq=seq, joined=joined), gr...  8.1 us
  transfers between devices with their start and end apart: 17, of which 8 were waited for; matrix products, arithmetic and copies ran while one was open for 1% of the time, Pallas kernels for 17%

profile of v1, /device:TPU:8, one launch (start us, length us, event | category | flops | bytes accessed | tf_op | source)
XLA Modules:
  0.0 211.2 jit_solution(15059397937360700633)
XLA Ops:
  3.8 13.8 %all_gather.3.taps_ref = f32[3,3,8192]{2,1,0:T(4,128)} all-gather(f32[3,3,1024]{2,1,0:T(4,128)} %param.12), channel_id=1, replica_groups=mesh['seq'=4,'ch'=8] {'ch'}, dimensions={2}, use_global_device_ids=true | all-gather | bytes 331776 | tf_op jit(solution)/shard_map/all_gather | solution.py:386
  17.6 5.3 %products.2 = (bf16[8,2,64,256]{3,2,1,0:T(8,128)(2,1)}, bf16[8,2,64,256]{3,2,1,0:T(8,128)(2,1)}, bf16[8,2,64,256]{3,2,1,0:T(8,128)(2,1)S(1)}, bf16[8,2,64,256]{3,2,1,0:T(8,128)(2,1)S(1)}) custom-call(s32[1]{0:T(128)} %bitcast.place_ref, bf16[4,3,64,8192]{3,2,1,0:T(8,128)(2,1)} %bitcast.3, bf16[4,3,64,8192]{3,2,1,0:T(8,128)(2,1)} %bitcast.4, ...), custom_call_target="tpu_custom_call" | custom-call | flops 20971520 | bytes 6291456 | tf_op jit(solution)/shard_map/products/pallas_call | solution.py:82
  28.0 37.1 %while.68 = (s32[]{:T(128)}, s32[1]{0:T(128)}, bf16[4,64,8192]{2,1,0:T(8,128)(2,1)}, bf16[8,2,64,256]{3,2,1,0:T(8,128)(2,1)}, bf16[8,2,64,256]{3,2,1,0:T(8,128)(...) while((s32[]{:T(128)}, s32[1]{0:T(128)}, ...), condition=%wide.region_1.0_spmd, body=%wide.region_0.0_spmd.sunk | while | flops 37748736 | bytes 25166008 | solution.py:375
  28.0 5.4 %products.3 = bf16[8,4,2,64,256]{4,3,2,1,0:T(8,128)(2,1)} custom-call(s32[1]{0:T(128)S(6)} %copy.15.refs_0_.place_ref.refs_1_, bf16[4,3,64,8192]{3,2,1,0:T(8,128)(2,1)} %get-tuple-element.631.query_ref.key_ref.value_ref, bf16[4,3,64,8192]{3,2,1,0:T(8,128)(2,1)} %get-tuple-element.631.query_ref.key_ref.value_ref, ...), custom_call_target="tpu_custom_call" | custom-call | flops 20971520 | bytes 6291456 | tf_op jit(solution)/shard_map/while/body/products/pallas_call | solution.py:82
  33.4 3.6 %all-to-all-start = ((bf16[8,4,2,64,256]{4,3,2,1,0:T(8,128)(2,1)}), bf16[8,4,2,64,256]{4,3,2,1,0:T(8,128)(2,1)S(1)}, u32[]{:S(2)}, u32[]{:S(2)}) async-start(bf16[8,4,2,64,256]{4,3,2,1,0:T(8,128)(2,1)} %products.3), calls=%async_computation | async-start | bytes 4194304 | tf_op jit(solution)/shard_map/while/body/all_to_all | solution.py:355
  37.0 6.1 %queries.1 = bf16[4,64,8192]{2,1,0:T(8,128)(2,1)} custom-call(bf16[4,3,64,8192]{3,2,1,0:T(8,128)(2,1)} %get-tuple-element.631.query_ref.key_ref.value_ref, bf16[4,3,2,8192]{3,2,1,0:T(2,128)(2,1)S(1)} %get-tuple-element.632.query_rim.key_rim.value_rim, f32[3,3,8192]{2,1,0:T(4,128)} %get-tuple-element.633.query_taps.taps_ref, s32[1]{0:T(128)S(6)} %copy.15.refs_0_.place_ref.refs_1_), custom_call_target="tpu_custom_call" | custom-call | flops 16777216 | bytes 8388608 | tf_op jit(solution)/shard_map/while/body/queries/pallas_call | solution.py:119
  43.1 20.5 %all-to-all-done.whole_ref = bf16[8,4,2,64,256]{4,3,2,1,0:T(8,128)(2,1)S(1)} async-done(((bf16[8,4,2,64,256]{4,3,2,1,0:T(8,128)(2,1)}), bf16[8,4,2,64,256]{4,3,2,1,0:T(8,128)(2,1)S(1)}, u32[]{:S(2)}, u32[]{:S(2)}) %all-to-all-start) | async-done | bytes 2097184 | tf_op jit(solution)/shard_map/while/body/all_to_all | solution.py:355
  69.1 3.9 %collective-permute-done.3 = bf16[8,2,64,256]{3,2,1,0:T(8,128)(2,1)} collective-permute-done((bf16[8,2,64,256]{3,2,1,0:T(8,128)(2,1)S(1)}, bf16[8,2,64,256]{3,2,1,0:T(8,128)(2,1)}, u32[]{:S(2)}, u32[]{:S(2)}) %collective-permute-start.3) | collective-permute-done | bytes 524320 | tf_op jit(solution)/shard_map/ppermute | solution.py:349
  73.0 39.1 %while.69 = (s32[]{:T(128)}, s32[1]{0:T(128)}, bf16[8,2,64,256]{3,2,1,0:T(8,128)(2,1)}, bf16[8,2,64,256]{3,2,1,0:T(8,128)(2,1)}, bf16[8,2,64,256]{3,2,1,0:T(8,12...) while((s32[]{:T(128)}, s32[1]{0:T(128)}, ...), condition=%wide.region_3.0_spmd, body=%wide.region_2.0_spmd.sunk | while | flops 2415919104 | bytes 15204541 | solution.py:375
  75.6 3.6 %all-to-all-start.1 = ((bf16[8,4,2,64,256]{4,3,2,1,0:T(8,128)(2,1)}), bf16[8,4,2,64,256]{4,3,2,1,0:T(8,128)(2,1)S(1)}, u32[]{:S(2)}, u32[]{:S(2)}) async-start(bf16[8,4,2,64,256]{4,3,2,1,0:T(8,128)(2,1)} %join.2), calls=%async_computation.1 | async-start | bytes 4194304 | tf_op jit(solution)/shard_map/while/body/all_to_all | solution.py:355
  79.2 26.6 %all-to-all-done.1.refs_0_ = bf16[8,4,2,64,256]{4,3,2,1,0:T(8,128)(2,1)S(1)} async-done(((bf16[8,4,2,64,256]{4,3,2,1,0:T(8,128)(2,1)}), bf16[8,4,2,64,256]{4,3,2,1,0:T(8,128)(2,1)S(1)}, u32[]{:S(2)}, u32[]{:S(2)}) %all-to-all-start.1) | async-done | bytes 2097184 | tf_op jit(solution)/shard_map/while/body/all_to_all | solution.py:355
  105.8 6.2 %long_conv.2 = (bf16[8,2,64,256]{3,2,1,0:T(8,128)(2,1)}, bf16[8,2,64,256]{3,2,1,0:T(8,128)(2,1)}, bf16[8,2,64,256]{3,2,1,0:T(8,128)(2,1)}, bf16[8,2,64,256]{3,2,1,0:T(8,128)(2,1)}) custom-call(s32[1]{0:T(128)S(6)} %copy.35.refs_4_.place_ref, bf16[8,4,2,64,256]{4,3,2,1,0:T(8,128)(2,1)S(1)} %all-to-all-done.1.refs_0_, f32[16,1,2048]{2,1,0:T(1,128)S(1)} %copy-done.1), custom_call_target="tpu_custom_call" | custom-call | flops 2415919104 | bytes 4194304 | tf_op jit(solution)/shard_map/while/body/long_conv/pallas_call | solution.py:230
  112.0 3.9 %collective-permute-start.5 = (bf16[8,2,64,256]{3,2,1,0:T(8,128)(2,1)}, bf16[8,2,64,256]{3,2,1,0:T(8,128)(2,1)}, u32[]{:S(2)}, u32[]{:S(2)}) collective-permute-start(bf16[8,2,64,256]{3,2,1,0:T(8,128)(2,1)} %get-tuple-element.251), channel_id=1, source_target_pairs={{0,16},{8,24},{16,0},{24,8},{1,17},{9,25},{17,1},{25,9},{2,18},{10... | collective-permute-start | bytes 1572872 | tf_op jit(solution)/shard_map/ppermute | solution.py:349
  118.0 39.4 %while.70 = (s32[]{:T(128)}, s32[1]{0:T(128)}, bf16[8,2,64,256]{3,2,1,0:T(8,128)(2,1)}, bf16[8,2,64,256]{3,2,1,0:T(8,128)(2,1)}, bf16[8,2,64,256]{3,2,1,0:T(8,12...) while((s32[]{:T(128)}, s32[1]{0:T(128)}, ...), condition=%wide.region_5.0_spmd, body=%wide.region_4.0_spmd.sunk | while | flops 2415919104 | bytes 23068852 | solution.py:375
  118.0 6.5 %long_conv.3 = bf16[8,4,2,64,256]{4,3,2,1,0:T(8,128)(2,1)S(1)} custom-call(s32[1]{0:T(128)} %get-tuple-element.682.place_ref, bf16[8,2,64,256]{3,2,1,0:T(8,128)(2,1)} %get-tuple-element.683.refs_0_, bf16[8,2,64,256]{3,2,1,0:T(8,128)(2,1)} %get-tuple-element.684.refs_1_, bf16[8,2,64,256]{3,2,1,0:T(8,128)(2,1)} %get-tuple-element.685.refs_2_, ...), custom_call_target="tpu_custom_call" | custom-call | flops 2415919104 | bytes 4194304 | tf_op jit(solution)/shard_map/while/body/long_conv/pallas_call | solution.py:230
  125.8 3.6 %all-to-all-start.2 = ((bf16[8,4,2,64,256]{4,3,2,1,0:T(8,128)(2,1)}), bf16[8,4,2,64,256]{4,3,2,1,0:T(8,128)(2,1)S(1)}, u32[]{:S(2)}, u32[]{:S(2)}) async-start(bf16[8,4,2,64,256]{4,3,2,1,0:T(8,128)(2,1)} %copy-done), calls=%async_computation.2 | async-start | bytes 4194304 | tf_op jit(solution)/shard_map/while/body/all_to_all | solution.py:355
  129.4 26.6 %all-to-all-done.2.whole_ref = bf16[8,4,2,64,256]{4,3,2,1,0:T(8,128)(2,1)S(1)} async-done(((bf16[8,4,2,64,256]{4,3,2,1,0:T(8,128)(2,1)}), bf16[8,4,2,64,256]{4,3,2,1,0:T(8,128)(2,1)S(1)}, u32[]{:S(2)}, u32[]{:S(2)}) %all-to-all-start.2) | async-done | bytes 2097184 | tf_op jit(solution)/shard_map/while/body/all_to_all | solution.py:355
  157.4 3.0 %collective-permute-start.11 = (bf16[8,2,64,256]{3,2,1,0:T(8,128)(2,1)}, bf16[8,2,64,256]{3,2,1,0:T(8,128)(2,1)S(1)}, u32[]{:S(2)}, u32[]{:S(2)}) collective-permute-start(bf16[8,2,64,256]{3,2,1,0:T(8,128)(2,1)} %get-tuple-element.259), channel_id=1, source_target_pairs={{0,16},{8,24},{16,0},{24,8},{1,17},{9,25},{17,1},{25,9},{2,18},{10... | collective-permute-start | bytes 1572872 | tf_op jit(solution)/shard_map/ppermute | solution.py:349
  163.0 36.7 %while.71 = (s32[]{:T(128)}, s32[1]{0:T(128)}, bf16[4,64,8192]{2,1,0:T(8,128)(2,1)}, s32[]{:T(128)}, bf16[8,2,64,256]{3,2,1,0:T(8,128)(2,1)}, /*index=5*/bf16[8,...) while((s32[]{:T(128)}, s32[1]{0:T(128)}, ...), condition=%wide.region_7.0_spmd, body=%wide.region_6.0_spmd.sunk | while | flops 1048579 | bytes 16777376 | solution.py:375
  165.6 3.6 %all-to-all-start.3 = ((bf16[8,4,2,64,256]{4,3,2,1,0:T(8,128)(2,1)}), bf16[8,4,2,64,256]{4,3,2,1,0:T(8,128)(2,1)S(1)}, u32[]{:S(2)}, u32[]{:S(2)}) async-start(bf16[8,4,2,64,256]{4,3,2,1,0:T(8,128)(2,1)} %join.3), calls=%async_computation.3 | async-start | bytes 4194304 | tf_op jit(solution)/shard_map/while/body/all_to_all | solution.py:355
  169.2 26.6 %all-to-all-done.3.refs_0_ = bf16[8,4,2,64,256]{4,3,2,1,0:T(8,128)(2,1)S(1)} async-done(((bf16[8,4,2,64,256]{4,3,2,1,0:T(8,128)(2,1)}), bf16[8,4,2,64,256]{4,3,2,1,0:T(8,128)(2,1)S(1)}, u32[]{:S(2)}, u32[]{:S(2)}) %all-to-all-start.3) | async-done | bytes 2097184 | tf_op jit(solution)/shard_map/while/body/all_to_all | solution.py:355
  195.8 4.0 %gate.3 = bf16[4,64,8192]{2,1,0:T(8,128)(2,1)} custom-call(s32[1]{0:T(128)S(6)} %copy.68.refs_4_.place_ref, bf16[4,64,8192]{2,1,0:T(8,128)(2,1)} %get-tuple-element.716.query_ref, bf16[8,4,2,64,256]{4,3,2,1,0:T(8,128)(2,1)S(1)} %all-to-all-done.3.refs_0_), custom_call_target="tpu_custom_call", output_to_operand_aliasing={{}: (1, {})} | custom-call | flops 1048576 | bytes 6291456 | tf_op jit(solution)/shard_map/while/body/gate/pallas_call | solution.py:326
  199.7 7.3 %collective-permute-done.12.refs_3_ = bf16[8,2,64,256]{3,2,1,0:T(8,128)(2,1)} collective-permute-done((bf16[8,2,64,256]{3,2,1,0:T(8,128)(2,1)}, bf16[8,2,64,256]{3,2,1,0:T(8,128)(2,1)}, u32[]{:S(2)}, u32[]{:S(2)}) %collective-permute-start.12) | collective-permute-done | bytes 524320 | tf_op jit(solution)/shard_map/ppermute | solution.py:349
  207.1 4.1 %gate.2 = bf16[4,64,8192]{2,1,0:T(8,128)(2,1)} custom-call(s32[1]{0:T(128)} %bitcast.place_ref, bf16[4,64,8192]{2,1,0:T(8,128)(2,1)} %get-tuple-element.257.query_ref, bf16[8,2,64,256]{3,2,1,0:T(8,128)(2,1)} %get-tuple-element.748, bf16[8,2,64,256]{3,2,1,0:T(8,128)(2,1)S(1)} %collective-permute-done.10.refs_1_, ...), custom_call_target="tpu_custom_call", output_to_operand_aliasing={{}: (1, {})} | custom-call | flops 1048576 | bytes 6291456 | tf_op jit(solution)/shard_map/gate/pallas_call | solution.py:326
  (34 shorter events, 27.0 us)
Async XLA Ops:
  1.9 15.7 %collective-permute-start = (bf16[4,2,3,8192]{3,1,2,0:T(2,128)(2,1)S(1)}, bf16[4,2,3,8192]{3,1,2,0:T(2,128)(2,1)S(1)}, u32[]{:S(2)}, u32[]{:S(2)}) collective-permute-start(bf16[4,2,3,8192]{3,1,2,0:T(2,128)(2,1)S(1)} %slice.3), channel_id=1, source_target_pairs={{0,1},{1,2},{2,3},{3,4},{4,5},{5,6},{6,7},{7,8},{8,9},{9,10},{10,1... | collective-permute-start | bytes 1179656 | tf_op jit(solution)/shard_map/ppermute | solution.py:18
  22.9 45.7 %collective-permute-start.1 = (bf16[8,2,64,256]{3,2,1,0:T(8,128)(2,1)}, bf16[8,2,64,256]{3,2,1,0:T(8,128)(2,1)}, u32[]{:S(2)}, u32[]{:S(2)}) collective-permute-start(bf16[8,2,64,256]{3,2,1,0:T(8,128)(2,1)} %get-tuple-element.245), channel_id=1, source_target_pairs={{0,8},{8,0},{16,24},{24,16},{1,9},{9,1},{17,25},{25,17},{2,10},{10... | collective-permute-start | bytes 1572872 | tf_op jit(solution)/shard_map/ppermute | solution.py:349
  23.3 45.8 %collective-permute-start.2 = (bf16[8,2,64,256]{3,2,1,0:T(8,128)(2,1)S(1)}, bf16[8,2,64,256]{3,2,1,0:T(8,128)(2,1)}, u32[]{:S(2)}, u32[]{:S(2)}) collective-permute-start(bf16[8,2,64,256]{3,2,1,0:T(8,128)(2,1)S(1)} %get-tuple-element.246), channel_id=1, source_target_pairs={{0,16},{8,24},{16,0},{24,8},{1,17},{9,25},{17,1},{25,9},{2,18},{10... | collective-permute-start | bytes 1572872 | tf_op jit(solution)/shard_map/ppermute | solution.py:349
  25.9 47.1 %collective-permute-start.3 = (bf16[8,2,64,256]{3,2,1,0:T(8,128)(2,1)S(1)}, bf16[8,2,64,256]{3,2,1,0:T(8,128)(2,1)}, u32[]{:S(2)}, u32[]{:S(2)}) collective-permute-start(bf16[8,2,64,256]{3,2,1,0:T(8,128)(2,1)S(1)} %get-tuple-element.247), channel_id=1, source_target_pairs={{0,24},{8,16},{16,8},{24,0},{1,25},{9,17},{17,9},{25,1},{2,26},{10... | collective-permute-start | bytes 1572872 | tf_op jit(solution)/shard_map/ppermute | solution.py:349
  33.4 30.2 %all-to-all-start = ((bf16[8,4,2,64,256]{4,3,2,1,0:T(8,128)(2,1)}), bf16[8,4,2,64,256]{4,3,2,1,0:T(8,128)(2,1)S(1)}, u32[]{:S(2)}, u32[]{:S(2)}) async-start(bf16[8,4,2,64,256]{4,3,2,1,0:T(8,128)(2,1)} %products.3), calls=%async_computation | async-start | bytes 4194304 | tf_op jit(solution)/shard_map/while/body/all_to_all | solution.py:355
  65.1 50.9 %collective-permute-start.7 = (bf16[8,2,64,256]{3,2,1,0:T(8,128)(2,1)}, bf16[8,2,64,256]{3,2,1,0:T(8,128)(2,1)}, u32[]{:S(2)}, u32[]{:S(2)}) collective-permute-start(bf16[8,2,64,256]{3,2,1,0:T(8,128)(2,1)} %get-tuple-element.253), channel_id=1, source_target_pairs={{0,8},{8,0},{16,24},{24,16},{1,9},{9,1},{17,25},{25,17},{2,10},{10... | collective-permute-start | bytes 1572872 | tf_op jit(solution)/shard_map/ppermute | solution.py:349
  66.4 49.7 %collective-permute-start.8 = (bf16[8,2,64,256]{3,2,1,0:T(8,128)(2,1)}, bf16[8,2,64,256]{3,2,1,0:T(8,128)(2,1)}, u32[]{:S(2)}, u32[]{:S(2)}) collective-permute-start(bf16[8,2,64,256]{3,2,1,0:T(8,128)(2,1)} %get-tuple-element.254), channel_id=1, source_target_pairs={{0,16},{8,24},{16,0},{24,8},{1,17},{9,25},{17,1},{25,9},{2,18},{10... | collective-permute-start | bytes 1572872 | tf_op jit(solution)/shard_map/ppermute | solution.py:349
  68.6 49.4 %collective-permute-start.9 = (bf16[8,2,64,256]{3,2,1,0:T(8,128)(2,1)}, bf16[8,2,64,256]{3,2,1,0:T(8,128)(2,1)}, u32[]{:S(2)}, u32[]{:S(2)}) collective-permute-start(bf16[8,2,64,256]{3,2,1,0:T(8,128)(2,1)} %get-tuple-element.255), channel_id=1, source_target_pairs={{0,24},{8,16},{16,8},{24,0},{1,25},{9,17},{17,9},{25,1},{2,26},{10... | collective-permute-start | bytes 1572872 | tf_op jit(solution)/shard_map/ppermute | solution.py:349
  73.0 32.8 %copy-start.1 = (f32[16,1,2048]{2,1,0:T(1,128)S(1)}, f32[16,1,2048]{2,1,0:T(1,128)}, u32[]{:S(2)}) copy-start(f32[16,1,2048]{2,1,0:T(1,128)} %get-tuple-element.667.refs_1_) | copy-start | bytes 393220 | tf_op jit(solution)/shard_map/while
  75.6 30.2 %all-to-all-start.1 = ((bf16[8,4,2,64,256]{4,3,2,1,0:T(8,128)(2,1)}), bf16[8,4,2,64,256]{4,3,2,1,0:T(8,128)(2,1)S(1)}, u32[]{:S(2)}, u32[]{:S(2)}) async-start(bf16[8,4,2,64,256]{4,3,2,1,0:T(8,128)(2,1)} %join.2), calls=%async_computation.1 | async-start | bytes 4194304 | tf_op jit(solution)/shard_map/while/body/all_to_all | solution.py:355
  112.0 48.3 %collective-permute-start.4 = (bf16[8,2,64,256]{3,2,1,0:T(8,128)(2,1)}, bf16[8,2,64,256]{3,2,1,0:T(8,128)(2,1)}, u32[]{:S(2)}, u32[]{:S(2)}) collective-permute-start(bf16[8,2,64,256]{3,2,1,0:T(8,128)(2,1)} %get-tuple-element.250), channel_id=1, source_target_pairs={{0,8},{8,0},{16,24},{24,16},{1,9},{9,1},{17,25},{25,17},{2,10},{10... | collective-permute-start | bytes 1572872 | tf_op jit(solution)/shard_map/ppermute | solution.py:349
  112.0 48.8 %collective-permute-start.5 = (bf16[8,2,64,256]{3,2,1,0:T(8,128)(2,1)}, bf16[8,2,64,256]{3,2,1,0:T(8,128)(2,1)}, u32[]{:S(2)}, u32[]{:S(2)}) collective-permute-start(bf16[8,2,64,256]{3,2,1,0:T(8,128)(2,1)} %get-tuple-element.251), channel_id=1, source_target_pairs={{0,16},{8,24},{16,0},{24,8},{1,17},{9,25},{17,1},{25,9},{2,18},{10... | collective-permute-start | bytes 1572872 | tf_op jit(solution)/shard_map/ppermute | solution.py:349
  116.0 47.0 %collective-permute-start.6 = (bf16[8,2,64,256]{3,2,1,0:T(8,128)(2,1)}, bf16[8,2,64,256]{3,2,1,0:T(8,128)(2,1)}, u32[]{:S(2)}, u32[]{:S(2)}) collective-permute-start(bf16[8,2,64,256]{3,2,1,0:T(8,128)(2,1)} %get-tuple-element.252), channel_id=1, source_target_pairs={{0,24},{8,16},{16,8},{24,0},{1,25},{9,17},{17,9},{25,1},{2,26},{10... | collective-permute-start | bytes 1572872 | tf_op jit(solution)/shard_map/ppermute | solution.py:349
  124.4 1.3 copy-start
  125.8 30.2 %all-to-all-start.2 = ((bf16[8,4,2,64,256]{4,3,2,1,0:T(8,128)(2,1)}), bf16[8,4,2,64,256]{4,3,2,1,0:T(8,128)(2,1)S(1)}, u32[]{:S(2)}, u32[]{:S(2)}) async-start(bf16[8,4,2,64,256]{4,3,2,1,0:T(8,128)(2,1)} %copy-done), calls=%async_computation.2 | async-start | bytes 4194304 | tf_op jit(solution)/shard_map/while/body/all_to_all | solution.py:355
  157.4 42.3 %collective-permute-start.10 = (bf16[8,2,64,256]{3,2,1,0:T(8,128)(2,1)}, bf16[8,2,64,256]{3,2,1,0:T(8,128)(2,1)S(1)}, u32[]{:S(2)}, u32[]{:S(2)}) collective-permute-start(bf16[8,2,64,256]{3,2,1,0:T(8,128)(2,1)} %get-tuple-element.258), channel_id=1, source_target_pairs={{0,8},{8,0},{16,24},{24,16},{1,9},{9,1},{17,25},{25,17},{2,10},{10... | collective-permute-start | bytes 1572872 | tf_op jit(solution)/shard_map/ppermute | solution.py:349
  157.4 42.3 %collective-permute-start.11 = (bf16[8,2,64,256]{3,2,1,0:T(8,128)(2,1)}, bf16[8,2,64,256]{3,2,1,0:T(8,128)(2,1)S(1)}, u32[]{:S(2)}, u32[]{:S(2)}) collective-permute-start(bf16[8,2,64,256]{3,2,1,0:T(8,128)(2,1)} %get-tuple-element.259), channel_id=1, source_target_pairs={{0,16},{8,24},{16,0},{24,8},{1,17},{9,25},{17,1},{25,9},{2,18},{10... | collective-permute-start | bytes 1572872 | tf_op jit(solution)/shard_map/ppermute | solution.py:349
  160.4 46.7 %collective-permute-start.12 = (bf16[8,2,64,256]{3,2,1,0:T(8,128)(2,1)}, bf16[8,2,64,256]{3,2,1,0:T(8,128)(2,1)}, u32[]{:S(2)}, u32[]{:S(2)}) collective-permute-start(bf16[8,2,64,256]{3,2,1,0:T(8,128)(2,1)} %get-tuple-element.260), channel_id=1, source_target_pairs={{0,24},{8,16},{16,8},{24,0},{1,25},{9,17},{17,9},{25,1},{2,26},{10... | collective-permute-start | bytes 1572872 | tf_op jit(solution)/shard_map/ppermute | solution.py:349
  165.6 30.2 %all-to-all-start.3 = ((bf16[8,4,2,64,256]{4,3,2,1,0:T(8,128)(2,1)}), bf16[8,4,2,64,256]{4,3,2,1,0:T(8,128)(2,1)S(1)}, u32[]{:S(2)}, u32[]{:S(2)}) async-start(bf16[8,4,2,64,256]{4,3,2,1,0:T(8,128)(2,1)} %join.3), calls=%async_computation.3 | async-start | bytes 4194304 | tf_op jit(solution)/shard_map/while/body/all_to_all | solution.py:355

commit v2 on v1

--- a/solution.py
+++ b/solution.py
@@ -33,65 +33,64 @@
     return total
 
 
-def product_kernel(place_ref, key_ref, value_ref, key_rim, value_rim, taps_ref, *refs, seq, outs):
+def product_kernel(place_ref, *refs, seq, outs):
+    if outs == 1:
+        product_body(place_ref[0], *refs, seq=seq, outs=outs)
+        return
+    for home in range(seq):
+        pl.when(place_ref[0] == home)(functools.partial(product_body, home, *refs, seq=seq, outs=outs))
+
+
+def product_body(place, key_ref, value_ref, key_rim, value_rim, taps_ref, *refs, seq, outs):
     shifted, outs = refs[-1], refs[-1 - outs : -1]
     count, width = key_ref.shape[0], outs[0].shape[-1]
     spans, lane = key_ref.shape[-1] // (seq * width), shifted.shape[-1]
-    for n in range(count):
-        for span in range(spans):
-            for part in range(seq):
-                for low in range(0, width, lane):
-                    start = (span * seq + part) * width + low
-                    if len(outs) > 1 and lane % 128 == 0:
-                        start = pl.multiple_of((span * seq + (place_ref[0] ^ part)) * width + low, lane)
-                    lanes = pl.ds(start, lane)
-                    keys = filtered_rows(
-                        shifted.at[0], key_ref[n, 0, :, lanes], key_rim[n, 0, :, lanes], taps_ref[:, 1, lanes]
-                    )
+    for span in range(spans):
+        for part in range(seq):
+            for low in range(0, width, lane):
+                start = (span * seq + part) * width + low
+                lanes = slice(start, start + lane)
+                key_taps, value_taps = taps_ref[:, 1, lanes], taps_ref[:, 2, lanes]
+                for n in range(count):
+                    keys = filtered_rows(shifted.at[2 * n], key_ref[n, 0, :, lanes], key_rim[n, 0, :, lanes], key_taps)
                     values = filtered_rows(
-                        shifted.at[1], value_ref[n, 0, :, lanes], value_rim[n, 0, :, lanes], taps_ref[:, 2, lanes]
+                        shifted.at[2 * n + 1], value_ref[n, 0, :, lanes], value_rim[n, 0, :, lanes], value_taps
                     )
                     product = (keys * values).astype(jnp.bfloat16)
                     if len(outs) == 1:
-                        outs[0][span, place_ref[0] ^ part, n, :, low : low + lane] = product
-                    elif lane % 128 == 0:
-                        outs[part][span, n, :, low : low + lane] = product
+                        outs[0][span, place ^ part, n, :, low : low + lane] = product
                     else:
-                        for step in range(seq):
-
-                            @pl.when((place_ref[0] ^ part) == step)
-                            def _(step=step, n=n, span=span, low=low, product=product):
-                                outs[step][span, n, :, low : low + lane] = product
+                        outs[place ^ part][span, n, :, low : low + lane] = product
 
 
 def products(place, proj, rim, taps, first, count, seq, ch, joined, after=()):
     rows, channels = proj.shape[2:]
     width = channels // (ch * seq)
-    spans = math.gcd(ch, 2)
-    block, start = spans * seq * width, first // count
+    spans = math.gcd(ch, 8)
+    block = spans * seq * width
 
     def of(component, depth):
-        return pl.BlockSpec((count, 1, depth, block), lambda j, *_: (start, component, 0, j))
+        return pl.BlockSpec((1, 1, depth, block), lambda n, j, *_: (first + n, component, 0, j))
 
     if joined:
-        out_specs = [pl.BlockSpec((spans, seq, count, rows, width), lambda j, *_: (j, 0, 0, 0, 0))]
+        out_specs = [pl.BlockSpec((spans, seq, 1, rows, width), lambda n, j, *_: (j, 0, n, 0, 0))]
         out_shape = [jax.ShapeDtypeStruct((ch, seq, count, rows, width), jnp.bfloat16)]
     else:
-        out_specs = [pl.BlockSpec((spans, count, rows, width), lambda j, *_: (j, 0, 0, 0))] * seq
+        out_specs = [pl.BlockSpec((spans, 1, rows, width), lambda n, j, *_: (j, n, 0, 0))] * seq
         out_shape = [jax.ShapeDtypeStruct((ch, count, rows, width), jnp.bfloat16)] * seq
     return pl.pallas_call(
         functools.partial(product_kernel, seq=seq, outs=len(out_shape)),
         grid_spec=pltpu.PrefetchScalarGridSpec(
             num_scalar_prefetch=1,
-            grid=(ch // spans,),
+            grid=(count, ch // spans),
             in_specs=[of(1, rows), of(2, rows), of(1, rim.shape[2]), of(2, rim.shape[2])]
-            + [pl.BlockSpec(taps.shape[:2] + (block,), lambda j, *_: (0, 0, j))]
+            + [pl.BlockSpec(taps.shape[:2] + (block,), lambda n, j, *_: (0, 0, j))]
             + [pl.BlockSpec(memory_space=pl.ANY)] * len(after),
             out_specs=out_specs,
-            scratch_shapes=[pltpu.VMEM((2, rows + 8, math.gcd(width, 128)), jnp.float32)],
+            scratch_shapes=[pltpu.VMEM((2 * count, rows + 8, math.gcd(width, 128)), jnp.float32)],
         ),
         out_shape=out_shape,
-        compiler_params=params(8, "arbitrary"),
+        compiler_params=params(14, "arbitrary", "arbitrary"),
         cost_estimate=pl.CostEstimate(
             flops=20 * count * rows * channels, bytes_accessed=6 * count * rows * channels, transcendentals=0
         ),
@@ -102,10 +101,11 @@
 def queries_kernel(query_ref, query_rim, query_taps, *refs):
     out_ref, shifted = refs[-2:]
     lane = shifted.shape[-1]
-    for n in range(query_ref.shape[0]):
-        for low in range(0, query_ref.shape[-1], lane):
-            lanes = slice(low, low + lane)
-            total = filtered_rows(shifted, query_ref[n, 0, :, lanes], query_rim[n, 0, :, lanes], query_taps[:, 0, lanes])
+    for low in range(0, query_ref.shape[-1], lane):
+        lanes = slice(low, low + lane)
+        taps = query_taps[:, 0, lanes]
+        for n in range(query_ref.shape[0]):
+            total = filtered_rows(shifted.at[n], query_ref[n, 0, :, lanes], query_rim[n, 0, :, lanes], taps)
             out_ref[n, :, lanes] = total.astype(jnp.bfloat16)
 
 
@@ -123,7 +123,7 @@
         + [pl.BlockSpec(memory_space=pl.ANY)] * len(after),
         out_specs=pl.BlockSpec((count, rows, block), lambda j: (0, 0, j)),
         out_shape=jax.ShapeDtypeStruct((count, rows, channels), jnp.bfloat16),
-        scratch_shapes=[pltpu.VMEM((rows + 8, math.gcd(block, 128)), jnp.float32)],
+        scratch_shapes=[pltpu.VMEM((count, rows + 8, math.gcd(block, 128)), jnp.float32)],
         compiler_params=params(8, "arbitrary"),
         cost_estimate=pl.CostEstimate(
             flops=8 * count * rows * channels, bytes_accessed=4 * count * rows * channels, transcendentals=0
@@ -343,6 +343,61 @@
     )(place, queries, *pieces)
 
 
+def half_gate_kernel(place_ref, queries_ref, *refs, first, half, far):
+    pieces, out_ref, query, gated, arrive, leave = refs[:half], *refs[-5:]
+    ch, count, _, width = pieces[0].shape
+    block = half * width
+
+    def column(c):
+        place = c * 2 + (lax.div(place_ref[0], half) ^ int(far))
+        return pl.ds(pl.multiple_of(place * block, block), block)
+
+    def inward(c):
+        source = queries_ref.at[pl.ds(first, count), :, column(c)]
+        return pltpu.make_async_copy(source, query.at[c], arrive.at[c])
+
+    def outward(c):
+        target = out_ref.at[pl.ds(first, count), :, column(c)]
+        return pltpu.make_async_copy(gated.at[c], target, leave.at[c])
+
+    for c in range(ch):
+        inward(c).start()
+    for c in range(ch):
+        inward(c).wait()
+        for home in range(half):
+
+            @pl.when(lax.rem(place_ref[0], half) == home)
+            def _(c=c, home=home):
+                for n in range(count):
+                    for part in range(half):
+                        lanes = slice(part * width, (part + 1) * width)
+                        value = query[c, n, :, lanes].astype(jnp.float32) * pieces[home ^ part][c, n].astype(jnp.float32)
+                        gated[c, n, :, lanes] = value.astype(jnp.bfloat16)
+
+        outward(c).start()
+    for c in range(ch):
+        outward(c).wait()
+
+
+def half_gate(place, queries, pieces, first, far):
+    half, (ch, count, rows, width) = len(pieces), pieces[0].shape
+    held = pltpu.VMEM((ch, count, rows, half * width), jnp.bfloat16)
+    return pl.pallas_call(
+        functools.partial(half_gate_kernel, first=first, half=half, far=far),
+        in_specs=[pl.BlockSpec(memory_space=pltpu.SMEM), pl.BlockSpec(memory_space=pl.ANY)]
+        + [pl.BlockSpec(memory_space=pltpu.VMEM)] * half,
+        out_specs=pl.BlockSpec(memory_space=pl.ANY),
+        out_shape=jax.ShapeDtypeStruct(queries.shape, jnp.bfloat16),
+        scratch_shapes=[held, held, pltpu.SemaphoreType.DMA((ch,)), pltpu.SemaphoreType.DMA((ch,))],
+        input_output_aliases={1: 0},
+        compiler_params=params(8),
+        cost_estimate=pl.CostEstimate(
+            flops=half * pieces[0].size, bytes_accessed=6 * half * pieces[0].size, transcendentals=0
+        ),
+        name="half_gate",
+    )(place, queries, *pieces)
+
+
 def swap(pieces):
     count = lax.axis_size("seq")
     return [
@@ -417,7 +472,9 @@
         return gate(place, queries, [spread(join(first, after=[place, second_back]))], 0, seq), *first
 
     out = staged(once, place, first_gate, queries, *swap(first))[0]
-    return gate(place, out, swap(second), half, seq)
+    second = swap(second)
+    out = half_gate(place, out, second[: seq // 2], half, False)
+    return half_gate(place, out, second[seq // 2 :], half, True)
 
 
 def solution(mesh):

time: 212 us -> 210 us (level)
  waiting for transfers between devices: 115 us -> 112 us
    pallas_call x0 -> x2, Pallas kernels: none -> 5.55 us  [half_gate(): pl.pallas_call(functools.partial(half_gate_kernel, first=first, half=half...]
    pallas_call x2 -> x1, Pallas kernels: 8.1 us -> 3.95 us  [gate(): pl.pallas_call(functools.partial(gate_kernel, seq=seq, joined=joined), gr...]
    ppermute x12, waiting for transfers between devices: 15.2 us -> 11.7 us  [swap(): lax.ppermute(piece, 'seq', [(source, source ^ step) for source in range(c...]
  transfers between devices with their start and end apart: 17 -> 17, of which waited for: 8 -> 8; matrix products, arithmetic and copies ran while one was open for 1% -> 1% of each run, Pallas kernels for 17% -> 19%
where the time goes in v2:
time: 210 us; the launch traced here: 209 us
  waiting for transfers between devices  112 us (53%)
  Pallas kernels  46.6 us (22%)
  starting transfers between devices  31.7 us (15%)
  blocking collectives  13.8 us (7%)
  local copies, waits for them, and re-layouts  3.93 us (2%)
    all_to_all x4, waiting for transfers between devices, spread(): return lax.all_to_all(whole, 'ch', split_axis=0, concat_axis=0, tiled=True)  100 us
    ppermute x12, starting transfers between devices, swap(): lax.ppermute(piece, 'seq', [(source, source ^ step) for source in range(c...  15.3 us
    all_to_all x4, starting transfers between devices, spread(): return lax.all_to_all(whole, 'ch', split_axis=0, concat_axis=0, tiled=True)  14.4 us
    all_gather x1, blocking collectives, shards(): taps = lax.all_gather(short_w, 'ch', axis=2, tiled=True)  13.8 us
    pallas_call x2, Pallas kernels, long_conv(): pl.pallas_call(functools.partial(conv_kernel, seq=seq, joined=joined), gr...  12.7 us
    ppermute x12, waiting for transfers between devices, swap(): lax.ppermute(piece, 'seq', [(source, source ^ step) for source in range(c...  11.7 us
    pallas_call x2, Pallas kernels, products(): pl.pallas_call(functools.partial(product_kernel, seq=seq, outs=len(out_sh...  10.3 us
    pallas_call x1, Pallas kernels, short_queries(): pl.pallas_call(queries_kernel, grid=(channels // block,), in_specs=[of(ro...  6.09 us
  transfers between devices with their start and end apart: 17, of which 8 were waited for; matrix products, arithmetic and copies ran while one was open for 1% of the time, Pallas kernels for 19%

profile of v2, /device:TPU:8, one launch (start us, length us, event | category | flops | bytes accessed | tf_op | source)
XLA Modules:
  0.0 209.0 jit_solution(14373161899955903362)
XLA Ops:
  3.8 13.8 %all_gather.3.refs_4_ = f32[3,3,8192]{2,1,0:T(4,128)} all-gather(f32[3,3,1024]{2,1,0:T(4,128)} %param.12), channel_id=1, replica_groups=mesh['seq'=4,'ch'=8] {'ch'}, dimensions={2}, use_global_device_ids=true | all-gather | bytes 331776 | tf_op jit(solution)/shard_map/all_gather | solution.py:441
  17.6 5.1 %products.2 = (bf16[8,2,64,256]{3,2,1,0:T(8,128)(2,1)}, bf16[8,2,64,256]{3,2,1,0:T(8,128)(2,1)}, bf16[8,2,64,256]{3,2,1,0:T(8,128)(2,1)S(1)}, bf16[8,2,64,256]{3,2,1,0:T(8,128)(2,1)S(1)}) custom-call(s32[1]{0:T(128)} %bitcast.place_ref, bf16[4,3,64,8192]{3,2,1,0:T(8,128)(2,1)} %bitcast.3, bf16[4,3,64,8192]{3,2,1,0:T(8,128)(2,1)} %bitcast.4, ...), custom_call_target="tpu_custom_call" | custom-call | flops 20971520 | bytes 6291456 | tf_op jit(solution)/shard_map/products/pallas_call | solution.py:81
  27.8 36.8 %while.68 = (s32[]{:T(128)}, s32[1]{0:T(128)}, bf16[4,64,8192]{2,1,0:T(8,128)(2,1)}, bf16[8,2,64,256]{3,2,1,0:T(8,128)(2,1)}, bf16[8,2,64,256]{3,2,1,0:T(8,128)(...) while((s32[]{:T(128)}, s32[1]{0:T(128)}, ...), condition=%wide.region_1.0_spmd, body=%wide.region_0.0_spmd.sunk | while | flops 37748736 | bytes 25166008 | solution.py:430
  27.8 5.2 %products.3 = bf16[8,4,2,64,256]{4,3,2,1,0:T(8,128)(2,1)} custom-call(s32[1]{0:T(128)S(6)} %copy.16.refs_0_.place_ref.refs_6_, bf16[4,3,64,8192]{3,2,1,0:T(8,128)(2,1)} %get-tuple-element.631.query_ref.refs_0_.refs_1_, bf16[4,3,64,8192]{3,2,1,0:T(8,128)(2,1)} %get-tuple-element.631.query_ref.refs_0_.refs_1_, ...), custom_call_target="tpu_custom_call" | custom-call | flops 20971520 | bytes 6291456 | tf_op jit(solution)/shard_map/while/body/products/pallas_call | solution.py:81
  32.9 3.6 %all-to-all-start = ((bf16[8,4,2,64,256]{4,3,2,1,0:T(8,128)(2,1)}), bf16[8,4,2,64,256]{4,3,2,1,0:T(8,128)(2,1)S(1)}, u32[]{:S(2)}, u32[]{:S(2)}) async-start(bf16[8,4,2,64,256]{4,3,2,1,0:T(8,128)(2,1)} %products.3), calls=%async_computation | async-start | bytes 4194304 | tf_op jit(solution)/shard_map/while/body/all_to_all | solution.py:410
  36.5 6.1 %queries.1 = bf16[4,64,8192]{2,1,0:T(8,128)(2,1)} custom-call(bf16[4,3,64,8192]{3,2,1,0:T(8,128)(2,1)} %get-tuple-element.631.query_ref.refs_0_.refs_1_, bf16[4,3,2,8192]{3,2,1,0:T(2,128)(2,1)S(1)} %get-tuple-element.632.query_rim.refs_2_.refs_3_, f32[3,3,8192]{2,1,0:T(4,128)} %get-tuple-element.633.query_taps.refs_4_, s32[1]{0:T(128)S(6)} %copy.16.refs_0_.place_ref.refs_6_), custom_call_target="tpu_custom_call" | custom-call | flops 16777216 | bytes 8388608 | tf_op jit(solution)/shard_map/while/body/queries/pallas_call | solution.py:119
  42.6 20.5 %all-to-all-done.whole_ref = bf16[8,4,2,64,256]{4,3,2,1,0:T(8,128)(2,1)S(1)} async-done(((bf16[8,4,2,64,256]{4,3,2,1,0:T(8,128)(2,1)}), bf16[8,4,2,64,256]{4,3,2,1,0:T(8,128)(2,1)S(1)}, u32[]{:S(2)}, u32[]{:S(2)}) %all-to-all-start) | async-done | bytes 2097184 | tf_op jit(solution)/shard_map/while/body/all_to_all | solution.py:410
  68.6 4.2 %collective-permute-done.3 = bf16[8,2,64,256]{3,2,1,0:T(8,128)(2,1)} collective-permute-done((bf16[8,2,64,256]{3,2,1,0:T(8,128)(2,1)S(1)}, bf16[8,2,64,256]{3,2,1,0:T(8,128)(2,1)}, u32[]{:S(2)}, u32[]{:S(2)}) %collective-permute-start.3) | collective-permute-done | bytes 524320 | tf_op jit(solution)/shard_map/ppermute | solution.py:404
  72.8 39.1 %while.69 = (s32[]{:T(128)}, s32[1]{0:T(128)}, bf16[8,2,64,256]{3,2,1,0:T(8,128)(2,1)}, bf16[8,2,64,256]{3,2,1,0:T(8,128)(2,1)}, bf16[8,2,64,256]{3,2,1,0:T(8,12...) while((s32[]{:T(128)}, s32[1]{0:T(128)}, ...), condition=%wide.region_3.0_spmd, body=%wide.region_2.0_spmd.sunk | while | flops 2415919104 | bytes 15204541 | solution.py:430
  75.4 3.6 %all-to-all-start.1 = ((bf16[8,4,2,64,256]{4,3,2,1,0:T(8,128)(2,1)}), bf16[8,4,2,64,256]{4,3,2,1,0:T(8,128)(2,1)S(1)}, u32[]{:S(2)}, u32[]{:S(2)}) async-start(bf16[8,4,2,64,256]{4,3,2,1,0:T(8,128)(2,1)} %join.2), calls=%async_computation.1 | async-start | bytes 4194304 | tf_op jit(solution)/shard_map/while/body/all_to_all | solution.py:410
  79.0 26.6 %all-to-all-done.1.refs_0_ = bf16[8,4,2,64,256]{4,3,2,1,0:T(8,128)(2,1)S(1)} async-done(((bf16[8,4,2,64,256]{4,3,2,1,0:T(8,128)(2,1)}), bf16[8,4,2,64,256]{4,3,2,1,0:T(8,128)(2,1)S(1)}, u32[]{:S(2)}, u32[]{:S(2)}) %all-to-all-start.1) | async-done | bytes 2097184 | tf_op jit(solution)/shard_map/while/body/all_to_all | solution.py:410
  105.6 6.2 %long_conv.2 = (bf16[8,2,64,256]{3,2,1,0:T(8,128)(2,1)}, bf16[8,2,64,256]{3,2,1,0:T(8,128)(2,1)}, bf16[8,2,64,256]{3,2,1,0:T(8,128)(2,1)}, bf16[8,2,64,256]{3,2,1,0:T(8,128)(2,1)}) custom-call(s32[1]{0:T(128)S(6)} %copy.36.refs_4_.place_ref, bf16[8,4,2,64,256]{4,3,2,1,0:T(8,128)(2,1)S(1)} %all-to-all-done.1.refs_0_, f32[16,1,2048]{2,1,0:T(1,128)S(1)} %copy-done.1), custom_call_target="tpu_custom_call" | custom-call | flops 2415919104 | bytes 4194304 | tf_op jit(solution)/shard_map/while/body/long_conv/pallas_call | solution.py:230
  111.8 4.3 %collective-permute-start.5 = (bf16[8,2,64,256]{3,2,1,0:T(8,128)(2,1)}, bf16[8,2,64,256]{3,2,1,0:T(8,128)(2,1)}, u32[]{:S(2)}, u32[]{:S(2)}) collective-permute-start(bf16[8,2,64,256]{3,2,1,0:T(8,128)(2,1)} %get-tuple-element.251), channel_id=1, source_target_pairs={{0,16},{8,24},{16,0},{24,8},{1,17},{9,25},{17,1},{25,9},{2,18},{10... | collective-permute-start | bytes 1572872 | tf_op jit(solution)/shard_map/ppermute | solution.py:404
  117.7 39.4 %while.70 = (s32[]{:T(128)}, s32[1]{0:T(128)}, bf16[8,2,64,256]{3,2,1,0:T(8,128)(2,1)}, bf16[8,2,64,256]{3,2,1,0:T(8,128)(2,1)}, bf16[8,2,64,256]{3,2,1,0:T(8,12...) while((s32[]{:T(128)}, s32[1]{0:T(128)}, ...), condition=%wide.region_5.0_spmd, body=%wide.region_4.0_spmd.sunk | while | flops 2415919104 | bytes 23068852 | solution.py:430
  117.7 6.5 %long_conv.3 = bf16[8,4,2,64,256]{4,3,2,1,0:T(8,128)(2,1)S(1)} custom-call(s32[1]{0:T(128)} %get-tuple-element.682.place_ref, bf16[8,2,64,256]{3,2,1,0:T(8,128)(2,1)} %get-tuple-element.683.refs_0_, bf16[8,2,64,256]{3,2,1,0:T(8,128)(2,1)} %get-tuple-element.684.refs_1_, bf16[8,2,64,256]{3,2,1,0:T(8,128)(2,1)} %get-tuple-element.685.refs_2_, ...), custom_call_target="tpu_custom_call" | custom-call | flops 2415919104 | bytes 4194304 | tf_op jit(solution)/shard_map/while/body/long_conv/pallas_call | solution.py:230
  125.5 3.6 %all-to-all-start.2 = ((bf16[8,4,2,64,256]{4,3,2,1,0:T(8,128)(2,1)}), bf16[8,4,2,64,256]{4,3,2,1,0:T(8,128)(2,1)S(1)}, u32[]{:S(2)}, u32[]{:S(2)}) async-start(bf16[8,4,2,64,256]{4,3,2,1,0:T(8,128)(2,1)} %copy-done), calls=%async_computation.2 | async-start | bytes 4194304 | tf_op jit(solution)/shard_map/while/body/all_to_all | solution.py:410
  129.1 26.6 %all-to-all-done.2.whole_ref = bf16[8,4,2,64,256]{4,3,2,1,0:T(8,128)(2,1)S(1)} async-done(((bf16[8,4,2,64,256]{4,3,2,1,0:T(8,128)(2,1)}), bf16[8,4,2,64,256]{4,3,2,1,0:T(8,128)(2,1)S(1)}, u32[]{:S(2)}, u32[]{:S(2)}) %all-to-all-start.2) | async-done | bytes 2097184 | tf_op jit(solution)/shard_map/while/body/all_to_all | solution.py:410
  157.1 3.0 %collective-permute-start.11 = (bf16[8,2,64,256]{3,2,1,0:T(8,128)(2,1)}, bf16[8,2,64,256]{3,2,1,0:T(8,128)(2,1)S(1)}, u32[]{:S(2)}, u32[]{:S(2)}) collective-permute-start(bf16[8,2,64,256]{3,2,1,0:T(8,128)(2,1)} %get-tuple-element.259), channel_id=1, source_target_pairs={{0,16},{8,24},{16,0},{24,8},{1,17},{9,25},{17,1},{25,9},{2,18},{10... | collective-permute-start | bytes 1572872 | tf_op jit(solution)/shard_map/ppermute | solution.py:404
  162.7 36.7 %while.71 = (s32[]{:T(128)}, s32[1]{0:T(128)}, bf16[4,64,8192]{2,1,0:T(8,128)(2,1)}, s32[]{:T(128)}, bf16[8,2,64,256]{3,2,1,0:T(8,128)(2,1)}, /*index=5*/bf16[8,...) while((s32[]{:T(128)}, s32[1]{0:T(128)}, ...), condition=%wide.region_7.0_spmd, body=%wide.region_6.0_spmd.sunk | while | flops 1048579 | bytes 16777376 | solution.py:430
  165.3 3.6 %all-to-all-start.3 = ((bf16[8,4,2,64,256]{4,3,2,1,0:T(8,128)(2,1)}), bf16[8,4,2,64,256]{4,3,2,1,0:T(8,128)(2,1)S(1)}, u32[]{:S(2)}, u32[]{:S(2)}) async-start(bf16[8,4,2,64,256]{4,3,2,1,0:T(8,128)(2,1)} %join.3), calls=%async_computation.3 | async-start | bytes 4194304 | tf_op jit(solution)/shard_map/while/body/all_to_all | solution.py:410
  168.9 26.6 %all-to-all-done.3.refs_0_ = bf16[8,4,2,64,256]{4,3,2,1,0:T(8,128)(2,1)S(1)} async-done(((bf16[8,4,2,64,256]{4,3,2,1,0:T(8,128)(2,1)}), bf16[8,4,2,64,256]{4,3,2,1,0:T(8,128)(2,1)S(1)}, u32[]{:S(2)}, u32[]{:S(2)}) %all-to-all-start.3) | async-done | bytes 2097184 | tf_op jit(solution)/shard_map/while/body/all_to_all | solution.py:410
  195.5 4.0 %gate.1 = bf16[4,64,8192]{2,1,0:T(8,128)(2,1)} custom-call(s32[1]{0:T(128)S(6)} %copy.69.refs_4_.place_ref, bf16[4,64,8192]{2,1,0:T(8,128)(2,1)} %get-tuple-element.716.query_ref, bf16[8,4,2,64,256]{4,3,2,1,0:T(8,128)(2,1)S(1)} %all-to-all-done.3.refs_0_), custom_call_target="tpu_custom_call", output_to_operand_aliasing={{}: (1, {})} | custom-call | flops 1048576 | bytes 6291456 | tf_op jit(solution)/shard_map/while/body/gate/pallas_call | solution.py:326
  199.4 3.4 %half_gate.2.queries_ref = bf16[4,64,8192]{2,1,0:T(8,128)(2,1)} custom-call(s32[1]{0:T(128)} %bitcast.place_ref, bf16[4,64,8192]{2,1,0:T(8,128)(2,1)} %get-tuple-element.257.queries_ref, bf16[8,2,64,256]{3,2,1,0:T(8,128)(2,1)} %get-tuple-element.748, bf16[8,2,64,256]{3,2,1,0:T(8,128)(2,1)} %collective-permute-done.10.refs_1_), custom_call_target="tpu_custom_call", output_to_operand_aliasing={{}: (1, {})} | custom-call | flops 524288 | bytes 3145728 | tf_op jit(solution)/shard_map/half_gate/pallas_call | solution.py:385
  202.8 3.9 %collective-permute-done.12.refs_1_ = bf16[8,2,64,256]{3,2,1,0:T(8,128)(2,1)S(1)} collective-permute-done((bf16[8,2,64,256]{3,2,1,0:T(8,128)(2,1)}, bf16[8,2,64,256]{3,2,1,0:T(8,128)(2,1)S(1)}, u32[]{:S(2)}, u32[]{:S(2)}) %collective-permute-start.12) | collective-permute-done | bytes 524320 | tf_op jit(solution)/shard_map/ppermute | solution.py:404
  (35 shorter events, 28.7 us)
Async XLA Ops:
  1.9 15.7 %collective-permute-start = (bf16[4,2,3,8192]{3,1,2,0:T(2,128)(2,1)S(1)}, bf16[4,2,3,8192]{3,1,2,0:T(2,128)(2,1)S(1)}, u32[]{:S(2)}, u32[]{:S(2)}) collective-permute-start(bf16[4,2,3,8192]{3,1,2,0:T(2,128)(2,1)S(1)} %slice.3), channel_id=1, source_target_pairs={{0,1},{1,2},{2,3},{3,4},{4,5},{5,6},{6,7},{7,8},{8,9},{9,10},{10,1... | collective-permute-start | bytes 1179656 | tf_op jit(solution)/shard_map/ppermute | solution.py:18
  22.7 45.4 %collective-permute-start.1 = (bf16[8,2,64,256]{3,2,1,0:T(8,128)(2,1)}, bf16[8,2,64,256]{3,2,1,0:T(8,128)(2,1)}, u32[]{:S(2)}, u32[]{:S(2)}) collective-permute-start(bf16[8,2,64,256]{3,2,1,0:T(8,128)(2,1)} %get-tuple-element.245), channel_id=1, source_target_pairs={{0,8},{8,0},{16,24},{24,16},{1,9},{9,1},{17,25},{25,17},{2,10},{10... | collective-permute-start | bytes 1572872 | tf_op jit(solution)/shard_map/ppermute | solution.py:404
  23.1 45.5 %collective-permute-start.2 = (bf16[8,2,64,256]{3,2,1,0:T(8,128)(2,1)S(1)}, bf16[8,2,64,256]{3,2,1,0:T(8,128)(2,1)}, u32[]{:S(2)}, u32[]{:S(2)}) collective-permute-start(bf16[8,2,64,256]{3,2,1,0:T(8,128)(2,1)S(1)} %get-tuple-element.246), channel_id=1, source_target_pairs={{0,16},{8,24},{16,0},{24,8},{1,17},{9,25},{17,1},{25,9},{2,18},{10... | collective-permute-start | bytes 1572872 | tf_op jit(solution)/shard_map/ppermute | solution.py:404
  25.7 47.1 %collective-permute-start.3 = (bf16[8,2,64,256]{3,2,1,0:T(8,128)(2,1)S(1)}, bf16[8,2,64,256]{3,2,1,0:T(8,128)(2,1)}, u32[]{:S(2)}, u32[]{:S(2)}) collective-permute-start(bf16[8,2,64,256]{3,2,1,0:T(8,128)(2,1)S(1)} %get-tuple-element.247), channel_id=1, source_target_pairs={{0,24},{8,16},{16,8},{24,0},{1,25},{9,17},{17,9},{25,1},{2,26},{10... | collective-permute-start | bytes 1572872 | tf_op jit(solution)/shard_map/ppermute | solution.py:404
  32.9 30.2 %all-to-all-start = ((bf16[8,4,2,64,256]{4,3,2,1,0:T(8,128)(2,1)}), bf16[8,4,2,64,256]{4,3,2,1,0:T(8,128)(2,1)S(1)}, u32[]{:S(2)}, u32[]{:S(2)}) async-start(bf16[8,4,2,64,256]{4,3,2,1,0:T(8,128)(2,1)} %products.3), calls=%async_computation | async-start | bytes 4194304 | tf_op jit(solution)/shard_map/while/body/all_to_all | solution.py:410
  64.6 51.6 %collective-permute-start.7 = (bf16[8,2,64,256]{3,2,1,0:T(8,128)(2,1)}, bf16[8,2,64,256]{3,2,1,0:T(8,128)(2,1)}, u32[]{:S(2)}, u32[]{:S(2)}) collective-permute-start(bf16[8,2,64,256]{3,2,1,0:T(8,128)(2,1)} %get-tuple-element.253), channel_id=1, source_target_pairs={{0,8},{8,0},{16,24},{24,16},{1,9},{9,1},{17,25},{25,17},{2,10},{10... | collective-permute-start | bytes 1572872 | tf_op jit(solution)/shard_map/ppermute | solution.py:404
  65.9 50.2 %collective-permute-start.8 = (bf16[8,2,64,256]{3,2,1,0:T(8,128)(2,1)}, bf16[8,2,64,256]{3,2,1,0:T(8,128)(2,1)}, u32[]{:S(2)}, u32[]{:S(2)}) collective-permute-start(bf16[8,2,64,256]{3,2,1,0:T(8,128)(2,1)} %get-tuple-element.254), channel_id=1, source_target_pairs={{0,16},{8,24},{16,0},{24,8},{1,17},{9,25},{17,1},{25,9},{2,18},{10... | collective-permute-start | bytes 1572872 | tf_op jit(solution)/shard_map/ppermute | solution.py:404
  68.0 49.7 %collective-permute-start.9 = (bf16[8,2,64,256]{3,2,1,0:T(8,128)(2,1)}, bf16[8,2,64,256]{3,2,1,0:T(8,128)(2,1)}, u32[]{:S(2)}, u32[]{:S(2)}) collective-permute-start(bf16[8,2,64,256]{3,2,1,0:T(8,128)(2,1)} %get-tuple-element.255), channel_id=1, source_target_pairs={{0,24},{8,16},{16,8},{24,0},{1,25},{9,17},{17,9},{25,1},{2,26},{10... | collective-permute-start | bytes 1572872 | tf_op jit(solution)/shard_map/ppermute | solution.py:404
  72.8 32.8 %copy-start.1 = (f32[16,1,2048]{2,1,0:T(1,128)S(1)}, f32[16,1,2048]{2,1,0:T(1,128)}, u32[]{:S(2)}) copy-start(f32[16,1,2048]{2,1,0:T(1,128)} %get-tuple-element.667.refs_1_) | copy-start | bytes 393220 | tf_op jit(solution)/shard_map/while
  75.4 30.2 %all-to-all-start.1 = ((bf16[8,4,2,64,256]{4,3,2,1,0:T(8,128)(2,1)}), bf16[8,4,2,64,256]{4,3,2,1,0:T(8,128)(2,1)S(1)}, u32[]{:S(2)}, u32[]{:S(2)}) async-start(bf16[8,4,2,64,256]{4,3,2,1,0:T(8,128)(2,1)} %join.2), calls=%async_computation.1 | async-start | bytes 4194304 | tf_op jit(solution)/shard_map/while/body/all_to_all | solution.py:410
  111.8 48.3 %collective-permute-start.4 = (bf16[8,2,64,256]{3,2,1,0:T(8,128)(2,1)}, bf16[8,2,64,256]{3,2,1,0:T(8,128)(2,1)}, u32[]{:S(2)}, u32[]{:S(2)}) collective-permute-start(bf16[8,2,64,256]{3,2,1,0:T(8,128)(2,1)} %get-tuple-element.250), channel_id=1, source_target_pairs={{0,8},{8,0},{16,24},{24,16},{1,9},{9,1},{17,25},{25,17},{2,10},{10... | collective-permute-start | bytes 1572872 | tf_op jit(solution)/shard_map/ppermute | solution.py:404
  111.8 48.8 %collective-permute-start.5 = (bf16[8,2,64,256]{3,2,1,0:T(8,128)(2,1)}, bf16[8,2,64,256]{3,2,1,0:T(8,128)(2,1)}, u32[]{:S(2)}, u32[]{:S(2)}) collective-permute-start(bf16[8,2,64,256]{3,2,1,0:T(8,128)(2,1)} %get-tuple-element.251), channel_id=1, source_target_pairs={{0,16},{8,24},{16,0},{24,8},{1,17},{9,25},{17,1},{25,9},{2,18},{10... | collective-permute-start | bytes 1572872 | tf_op jit(solution)/shard_map/ppermute | solution.py:404
  116.1 46.6 %collective-permute-start.6 = (bf16[8,2,64,256]{3,2,1,0:T(8,128)(2,1)}, bf16[8,2,64,256]{3,2,1,0:T(8,128)(2,1)}, u32[]{:S(2)}, u32[]{:S(2)}) collective-permute-start(bf16[8,2,64,256]{3,2,1,0:T(8,128)(2,1)} %get-tuple-element.252), channel_id=1, source_target_pairs={{0,24},{8,16},{16,8},{24,0},{1,25},{9,17},{17,9},{25,1},{2,26},{10... | collective-permute-start | bytes 1572872 | tf_op jit(solution)/shard_map/ppermute | solution.py:404
  124.2 1.3 copy-start
  125.5 30.2 %all-to-all-start.2 = ((bf16[8,4,2,64,256]{4,3,2,1,0:T(8,128)(2,1)}), bf16[8,4,2,64,256]{4,3,2,1,0:T(8,128)(2,1)S(1)}, u32[]{:S(2)}, u32[]{:S(2)}) async-start(bf16[8,4,2,64,256]{4,3,2,1,0:T(8,128)(2,1)} %copy-done), calls=%async_computation.2 | async-start | bytes 4194304 | tf_op jit(solution)/shard_map/while/body/all_to_all | solution.py:410
  157.1 42.4 %collective-permute-start.10 = (bf16[8,2,64,256]{3,2,1,0:T(8,128)(2,1)}, bf16[8,2,64,256]{3,2,1,0:T(8,128)(2,1)}, u32[]{:S(2)}, u32[]{:S(2)}) collective-permute-start(bf16[8,2,64,256]{3,2,1,0:T(8,128)(2,1)} %get-tuple-element.258), channel_id=1, source_target_pairs={{0,8},{8,0},{16,24},{24,16},{1,9},{9,1},{17,25},{25,17},{2,10},{10... | collective-permute-start | bytes 1572872 | tf_op jit(solution)/shard_map/ppermute | solution.py:404
  157.1 45.7 %collective-permute-start.11 = (bf16[8,2,64,256]{3,2,1,0:T(8,128)(2,1)}, bf16[8,2,64,256]{3,2,1,0:T(8,128)(2,1)S(1)}, u32[]{:S(2)}, u32[]{:S(2)}) collective-permute-start(bf16[8,2,64,256]{3,2,1,0:T(8,128)(2,1)} %get-tuple-element.259), channel_id=1, source_target_pairs={{0,16},{8,24},{16,0},{24,8},{1,17},{9,25},{17,1},{25,9},{2,18},{10... | collective-permute-start | bytes 1572872 | tf_op jit(solution)/shard_map/ppermute | solution.py:404
  160.1 46.6 %collective-permute-start.12 = (bf16[8,2,64,256]{3,2,1,0:T(8,128)(2,1)}, bf16[8,2,64,256]{3,2,1,0:T(8,128)(2,1)S(1)}, u32[]{:S(2)}, u32[]{:S(2)}) collective-permute-start(bf16[8,2,64,256]{3,2,1,0:T(8,128)(2,1)} %get-tuple-element.260), channel_id=1, source_target_pairs={{0,24},{8,16},{16,8},{24,0},{1,25},{9,17},{17,9},{25,1},{2,26},{10... | collective-permute-start | bytes 1572872 | tf_op jit(solution)/shard_map/ppermute | solution.py:404
  165.3 30.2 %all-to-all-start.3 = ((bf16[8,4,2,64,256]{4,3,2,1,0:T(8,128)(2,1)}), bf16[8,4,2,64,256]{4,3,2,1,0:T(8,128)(2,1)S(1)}, u32[]{:S(2)}, u32[]{:S(2)}) async-start(bf16[8,4,2,64,256]{4,3,2,1,0:T(8,128)(2,1)} %join.3), calls=%async_computation.3 | async-start | bytes 4194304 | tf_op jit(solution)/shard_map/while/body/all_to_all | solution.py:410

commit v3 on v2

--- a/solution.py
+++ b/solution.py
@@ -398,6 +398,51 @@
     )(place, queries, *pieces)
 
 
+def step_gate_kernel(place_ref, queries_ref, piece_ref, *refs, first, step, seq):
+    out_ref, query, gated, arrive, leave = refs
+    ch, count, _, width = piece_ref.shape
+
+    def column(c):
+        return pl.ds(pl.multiple_of((c * seq + (place_ref[0] ^ step)) * width, width), width)
+
+    def inward(c):
+        source = queries_ref.at[pl.ds(first, count), :, column(c)]
+        return pltpu.make_async_copy(source, query.at[c], arrive.at[c])
+
+    def outward(c):
+        target = out_ref.at[pl.ds(first, count), :, column(c)]
+        return pltpu.make_async_copy(gated.at[c], target, leave.at[c])
+
+    for c in range(ch):
+        inward(c).start()
+    for c in range(ch):
+        inward(c).wait()
+        gated[c] = (query[c].astype(jnp.float32) * piece_ref[c].astype(jnp.float32)).astype(jnp.bfloat16)
+        outward(c).start()
+    for c in range(ch):
+        outward(c).wait()
+
+
+def step_gate(place, queries, piece, first, step, seq):
+    held = pltpu.VMEM(piece.shape, jnp.bfloat16)
+    semaphores = pltpu.SemaphoreType.DMA(piece.shape[:1])
+    return pl.pallas_call(
+        functools.partial(step_gate_kernel, first=first, step=step, seq=seq),
+        in_specs=[
+            pl.BlockSpec(memory_space=pltpu.SMEM),
+            pl.BlockSpec(memory_space=pl.ANY),
+            pl.BlockSpec(memory_space=pltpu.VMEM),
+        ],
+        out_specs=pl.BlockSpec(memory_space=pl.ANY),
+        out_shape=jax.ShapeDtypeStruct(queries.shape, jnp.bfloat16),
+        scratch_shapes=[held, held, semaphores, semaphores],
+        input_output_aliases={1: 0},
+        compiler_params=params(8),
+        cost_estimate=pl.CostEstimate(flops=piece.size, bytes_accessed=6 * piece.size, transcendentals=0),
+        name="step_gate",
+    )(place, queries, piece)
+
+
 def swap(pieces):
     count = lax.axis_size("seq")
     return [
@@ -456,9 +501,10 @@
     second_sent = second[0]
 
     def first_turn(place, *first):
-        return long_conv(place, [spread(join(first, after=[place, second_sent]))], filters, seq)
-
-    first = staged(once, place, first_turn, *swap(first))
+        whole = spread(join(first[::-1], after=[place, second_sent]))
+        return long_conv(place, [whole], filters, seq)[::-1]
+
+    first = staged(once, place, first_turn, *swap(first)[::-1])[::-1]
     first_sent = first[0]
 
     def second_turn(place, *second):
@@ -474,7 +520,11 @@
     out = staged(once, place, first_gate, queries, *swap(first))[0]
     second = swap(second)
     out = half_gate(place, out, second[: seq // 2], half, False)
-    return half_gate(place, out, second[seq // 2 :], half, True)
+    if second[0].shape[-1] % 128:
+        return half_gate(place, out, second[seq // 2 :], half, True)
+    for step in range(seq // 2, seq):
+        out = step_gate(place, out, second[step], half, step, seq)
+    return out
 
 
 def solution(mesh):

time: 210 us -> 209 us (level)
  waiting for transfers between devices: 112 us -> 109 us
    pallas_call x0 -> x2, Pallas kernels: none -> 3.71 us  [step_gate(): pl.pallas_call(functools.partial(step_gate_kernel, first=first, step=step...]
    ppermute x12, waiting for transfers between devices: 11.7 us -> 9.03 us  [swap(): lax.ppermute(piece, 'seq', [(source, source ^ step) for source in range(c...]
    pallas_call x2 -> x1, Pallas kernels: 5.55 us -> 3.37 us  [half_gate(): pl.pallas_call(functools.partial(half_gate_kernel, first=first, half=half...]
  transfers between devices with their start and end apart: 17 -> 17, of which waited for: 8 -> 8; matrix products, arithmetic and copies ran while one was open for 1% -> 1% of each run, Pallas kernels for 19% -> 20%
where the time goes in v3:
time: 209 us; the launch traced here: 208 us
  waiting for transfers between devices  109 us (52%)
  Pallas kernels  48.2 us (23%)
  starting transfers between devices  31.5 us (15%)
  blocking collectives  13.8 us (7%)
  local copies, waits for them, and re-layouts  3.93 us (2%)
    all_to_all x4, waiting for transfers between devices, spread(): return lax.all_to_all(whole, 'ch', split_axis=0, concat_axis=0, tiled=True)  100 us
    ppermute x12, starting transfers between devices, swap(): lax.ppermute(piece, 'seq', [(source, source ^ step) for source in range(c...  15.2 us
    all_to_all x4, starting transfers between devices, spread(): return lax.all_to_all(whole, 'ch', split_axis=0, concat_axis=0, tiled=True)  14.4 us
    all_gather x1, blocking collectives, shards(): taps = lax.all_gather(short_w, 'ch', axis=2, tiled=True)  13.8 us
    pallas_call x2, Pallas kernels, long_conv(): pl.pallas_call(functools.partial(conv_kernel, seq=seq, joined=joined), gr...  12.7 us
    pallas_call x2, Pallas kernels, products(): pl.pallas_call(functools.partial(product_kernel, seq=seq, outs=len(out_sh...  10.3 us
    ppermute x12, waiting for transfers between devices, swap(): lax.ppermute(piece, 'seq', [(source, source ^ step) for source in range(c...  9.03 us
    pallas_call x1, Pallas kernels, short_queries(): pl.pallas_call(queries_kernel, grid=(channels // block,), in_specs=[of(ro...  6.09 us
  transfers between devices with their start and end apart: 17, of which 8 were waited for; matrix products, arithmetic and copies ran while one was open for 1% of the time, Pallas kernels for 20%

profile of v3, /device:TPU:8, one launch (start us, length us, event | category | flops | bytes accessed | tf_op | source)
XLA Modules:
  0.0 207.7 jit_solution(10025973143813666336)
XLA Ops:
  3.8 13.8 %all_gather.3.refs_4_ = f32[3,3,8192]{2,1,0:T(4,128)} all-gather(f32[3,3,1024]{2,1,0:T(4,128)} %param.12), channel_id=1, replica_groups=mesh['seq'=4,'ch'=8] {'ch'}, dimensions={2}, use_global_device_ids=true | all-gather | bytes 331776 | tf_op jit(solution)/shard_map/all_gather | solution.py:486
  17.6 5.1 %products.2 = (bf16[8,2,64,256]{3,2,1,0:T(8,128)(2,1)}, bf16[8,2,64,256]{3,2,1,0:T(8,128)(2,1)S(1)}, bf16[8,2,64,256]{3,2,1,0:T(8,128)(2,1)S(1)}, bf16[8,2,64,256]{3,2,1,0:T(8,128)(2,1)}) custom-call(s32[1]{0:T(128)} %bitcast.place_ref, bf16[4,3,64,8192]{3,2,1,0:T(8,128)(2,1)} %bitcast.3, bf16[4,3,64,8192]{3,2,1,0:T(8,128)(2,1)} %bitcast.4, ...), custom_call_target="tpu_custom_call" | custom-call | flops 20971520 | bytes 6291456 | tf_op jit(solution)/shard_map/products/pallas_call | solution.py:81
  28.3 36.8 %while.68 = (s32[]{:T(128)}, s32[1]{0:T(128)}, bf16[4,64,8192]{2,1,0:T(8,128)(2,1)}, bf16[8,2,64,256]{3,2,1,0:T(8,128)(2,1)}, bf16[8,2,64,256]{3,2,1,0:T(8,128)(...) while((s32[]{:T(128)}, s32[1]{0:T(128)}, ...), condition=%wide.region_1.0_spmd, body=%wide.region_0.0_spmd.sunk | while | flops 37748736 | bytes 25166008 | solution.py:475
  28.3 5.2 %products.3 = bf16[8,4,2,64,256]{4,3,2,1,0:T(8,128)(2,1)} custom-call(s32[1]{0:T(128)S(6)} %copy.17.refs_0_.place_ref.refs_6_, bf16[4,3,64,8192]{3,2,1,0:T(8,128)(2,1)} %get-tuple-element.631.query_ref.refs_0_.refs_1_, bf16[4,3,64,8192]{3,2,1,0:T(8,128)(2,1)} %get-tuple-element.631.query_ref.refs_0_.refs_1_, ...), custom_call_target="tpu_custom_call" | custom-call | flops 20971520 | bytes 6291456 | tf_op jit(solution)/shard_map/while/body/products/pallas_call | solution.py:81
  33.5 3.6 %all-to-all-start = ((bf16[8,4,2,64,256]{4,3,2,1,0:T(8,128)(2,1)}), bf16[8,4,2,64,256]{4,3,2,1,0:T(8,128)(2,1)S(1)}, u32[]{:S(2)}, u32[]{:S(2)}) async-start(bf16[8,4,2,64,256]{4,3,2,1,0:T(8,128)(2,1)} %products.3), calls=%async_computation | async-start | bytes 4194304 | tf_op jit(solution)/shard_map/while/body/all_to_all | solution.py:455
  37.1 6.1 %queries.1 = bf16[4,64,8192]{2,1,0:T(8,128)(2,1)} custom-call(bf16[4,3,64,8192]{3,2,1,0:T(8,128)(2,1)} %get-tuple-element.631.query_ref.refs_0_.refs_1_, bf16[4,3,2,8192]{3,2,1,0:T(2,128)(2,1)S(1)} %get-tuple-element.632.query_rim.refs_2_.refs_3_, f32[3,3,8192]{2,1,0:T(4,128)} %get-tuple-element.633.query_taps.refs_4_, s32[1]{0:T(128)S(6)} %copy.17.refs_0_.place_ref.refs_6_), custom_call_target="tpu_custom_call" | custom-call | flops 16777216 | bytes 8388608 | tf_op jit(solution)/shard_map/while/body/queries/pallas_call | solution.py:119
  43.2 20.5 %all-to-all-done.whole_ref = bf16[8,4,2,64,256]{4,3,2,1,0:T(8,128)(2,1)S(1)} async-done(((bf16[8,4,2,64,256]{4,3,2,1,0:T(8,128)(2,1)}), bf16[8,4,2,64,256]{4,3,2,1,0:T(8,128)(2,1)S(1)}, u32[]{:S(2)}, u32[]{:S(2)}) %all-to-all-start) | async-done | bytes 2097184 | tf_op jit(solution)/shard_map/while/body/all_to_all | solution.py:455
  70.5 39.1 %while.69 = (s32[]{:T(128)}, s32[1]{0:T(128)}, bf16[8,2,64,256]{3,2,1,0:T(8,128)(2,1)}, bf16[8,2,64,256]{3,2,1,0:T(8,128)(2,1)}, bf16[8,2,64,256]{3,2,1,0:T(8,12...) while((s32[]{:T(128)}, s32[1]{0:T(128)}, ...), condition=%wide.region_3.0_spmd, body=%wide.region_2.0_spmd.sunk | while | flops 2415919104 | bytes 15204541 | solution.py:475
  70.5 2.6 %join.2 = bf16[8,4,2,64,256]{4,3,2,1,0:T(8,128)(2,1)} custom-call(bf16[8,2,64,256]{3,2,1,0:T(8,128)(2,1)} %get-tuple-element.653.refs_0_, bf16[8,2,64,256]{3,2,1,0:T(8,128)(2,1)} %get-tuple-element.652.refs_1_, bf16[8,2,64,256]{3,2,1,0:T(8,128)(2,1)} %get-tuple-element.651.refs_2_, bf16[8,2,64,256]{3,2,1,0:T(8,128)(2,1)} %get-tuple-element.650.refs_3_, ...), custom_call_target="tpu_custom_call" | custom-call | bytes 4194304 | tf_op jit(solution)/shard_map/while/body/join/pallas_call | solution.py:261
  73.1 3.6 %all-to-all-start.1 = ((bf16[8,4,2,64,256]{4,3,2,1,0:T(8,128)(2,1)}), bf16[8,4,2,64,256]{4,3,2,1,0:T(8,128)(2,1)S(1)}, u32[]{:S(2)}, u32[]{:S(2)}) async-start(bf16[8,4,2,64,256]{4,3,2,1,0:T(8,128)(2,1)} %join.2), calls=%async_computation.1 | async-start | bytes 4194304 | tf_op jit(solution)/shard_map/while/body/all_to_all | solution.py:455
  76.7 26.6 %all-to-all-done.1.refs_0_ = bf16[8,4,2,64,256]{4,3,2,1,0:T(8,128)(2,1)S(1)} async-done(((bf16[8,4,2,64,256]{4,3,2,1,0:T(8,128)(2,1)}), bf16[8,4,2,64,256]{4,3,2,1,0:T(8,128)(2,1)S(1)}, u32[]{:S(2)}, u32[]{:S(2)}) %all-to-all-start.1) | async-done | bytes 2097184 | tf_op jit(solution)/shard_map/while/body/all_to_all | solution.py:455
  103.3 6.2 %long_conv.2 = (bf16[8,2,64,256]{3,2,1,0:T(8,128)(2,1)}, bf16[8,2,64,256]{3,2,1,0:T(8,128)(2,1)}, bf16[8,2,64,256]{3,2,1,0:T(8,128)(2,1)}, bf16[8,2,64,256]{3,2,1,0:T(8,128)(2,1)}) custom-call(s32[1]{0:T(128)S(6)} %copy.37.refs_4_.place_ref, bf16[8,4,2,64,256]{4,3,2,1,0:T(8,128)(2,1)S(1)} %all-to-all-done.1.refs_0_, f32[16,1,2048]{2,1,0:T(1,128)S(1)} %copy-done.1), custom_call_target="tpu_custom_call" | custom-call | flops 2415919104 | bytes 4194304 | tf_op jit(solution)/shard_map/while/body/long_conv/pallas_call | solution.py:230
  113.7 2.8 %collective-permute-done.9 = bf16[8,2,64,256]{3,2,1,0:T(8,128)(2,1)} collective-permute-done((bf16[8,2,64,256]{3,2,1,0:T(8,128)(2,1)}, bf16[8,2,64,256]{3,2,1,0:T(8,128)(2,1)}, u32[]{:S(2)}, u32[]{:S(2)}) %collective-permute-start.9) | collective-permute-done | bytes 524320 | tf_op jit(solution)/shard_map/ppermute | solution.py:449
  116.4 39.4 %while.70 = (s32[]{:T(128)}, s32[1]{0:T(128)}, bf16[8,2,64,256]{3,2,1,0:T(8,128)(2,1)}, bf16[8,2,64,256]{3,2,1,0:T(8,128)(2,1)}, bf16[8,2,64,256]{3,2,1,0:T(8,12...) while((s32[]{:T(128)}, s32[1]{0:T(128)}, ...), condition=%wide.region_5.0_spmd, body=%wide.region_4.0_spmd.sunk | while | flops 2415919104 | bytes 23068852 | solution.py:475
  116.4 6.5 %long_conv.3 = bf16[8,4,2,64,256]{4,3,2,1,0:T(8,128)(2,1)S(1)} custom-call(s32[1]{0:T(128)} %get-tuple-element.682.place_ref, bf16[8,2,64,256]{3,2,1,0:T(8,128)(2,1)} %get-tuple-element.683.refs_0_, bf16[8,2,64,256]{3,2,1,0:T(8,128)(2,1)} %get-tuple-element.684.refs_1_, bf16[8,2,64,256]{3,2,1,0:T(8,128)(2,1)} %get-tuple-element.685.refs_2_, ...), custom_call_target="tpu_custom_call" | custom-call | flops 2415919104 | bytes 4194304 | tf_op jit(solution)/shard_map/while/body/long_conv/pallas_call | solution.py:230
  124.2 3.6 %all-to-all-start.2 = ((bf16[8,4,2,64,256]{4,3,2,1,0:T(8,128)(2,1)}), bf16[8,4,2,64,256]{4,3,2,1,0:T(8,128)(2,1)S(1)}, u32[]{:S(2)}, u32[]{:S(2)}) async-start(bf16[8,4,2,64,256]{4,3,2,1,0:T(8,128)(2,1)} %copy-done), calls=%async_computation.2 | async-start | bytes 4194304 | tf_op jit(solution)/shard_map/while/body/all_to_all | solution.py:455
  127.8 26.6 %all-to-all-done.2.whole_ref = bf16[8,4,2,64,256]{4,3,2,1,0:T(8,128)(2,1)S(1)} async-done(((bf16[8,4,2,64,256]{4,3,2,1,0:T(8,128)(2,1)}), bf16[8,4,2,64,256]{4,3,2,1,0:T(8,128)(2,1)S(1)}, u32[]{:S(2)}, u32[]{:S(2)}) %all-to-all-start.2) | async-done | bytes 2097184 | tf_op jit(solution)/shard_map/while/body/all_to_all | solution.py:455
  155.9 3.0 %collective-permute-start.11 = (bf16[8,2,64,256]{3,2,1,0:T(8,128)(2,1)}, bf16[8,2,64,256]{3,2,1,0:T(8,128)(2,1)S(1)}, u32[]{:S(2)}, u32[]{:S(2)}) collective-permute-start(bf16[8,2,64,256]{3,2,1,0:T(8,128)(2,1)} %get-tuple-element.259), channel_id=1, source_target_pairs={{0,16},{8,24},{16,0},{24,8},{1,17},{9,25},{17,1},{25,9},{2,18},{10... | collective-permute-start | bytes 1572872 | tf_op jit(solution)/shard_map/ppermute | solution.py:449
  161.4 36.7 %while.71 = (s32[]{:T(128)}, s32[1]{0:T(128)}, bf16[4,64,8192]{2,1,0:T(8,128)(2,1)}, s32[]{:T(128)}, bf16[8,2,64,256]{3,2,1,0:T(8,128)(2,1)}, /*index=5*/bf16[8,...) while((s32[]{:T(128)}, s32[1]{0:T(128)}, ...), condition=%wide.region_7.0_spmd, body=%wide.region_6.0_spmd.sunk | while | flops 1048579 | bytes 16777376 | solution.py:475
  161.4 2.6 %join.3 = bf16[8,4,2,64,256]{4,3,2,1,0:T(8,128)(2,1)} custom-call(bf16[8,2,64,256]{3,2,1,0:T(8,128)(2,1)} %get-tuple-element.729.refs_0_, bf16[8,2,64,256]{3,2,1,0:T(8,128)(2,1)} %get-tuple-element.730.refs_1_, bf16[8,2,64,256]{3,2,1,0:T(8,128)(2,1)} %get-tuple-element.731.refs_2_, bf16[8,2,64,256]{3,2,1,0:T(8,128)(2,1)} %get-tuple-element.732.refs_3_, ...), custom_call_target="tpu_custom_call" | custom-call | bytes 4194304 | tf_op jit(solution)/shard_map/while/body/join/pallas_call | solution.py:261
  164.0 3.6 %all-to-all-start.3 = ((bf16[8,4,2,64,256]{4,3,2,1,0:T(8,128)(2,1)}), bf16[8,4,2,64,256]{4,3,2,1,0:T(8,128)(2,1)S(1)}, u32[]{:S(2)}, u32[]{:S(2)}) async-start(bf16[8,4,2,64,256]{4,3,2,1,0:T(8,128)(2,1)} %join.3), calls=%async_computation.3 | async-start | bytes 4194304 | tf_op jit(solution)/shard_map/while/body/all_to_all | solution.py:455
  167.6 26.6 %all-to-all-done.3.refs_0_ = bf16[8,4,2,64,256]{4,3,2,1,0:T(8,128)(2,1)S(1)} async-done(((bf16[8,4,2,64,256]{4,3,2,1,0:T(8,128)(2,1)}), bf16[8,4,2,64,256]{4,3,2,1,0:T(8,128)(2,1)S(1)}, u32[]{:S(2)}, u32[]{:S(2)}) %all-to-all-start.3) | async-done | bytes 2097184 | tf_op jit(solution)/shard_map/while/body/all_to_all | solution.py:455
  194.2 4.0 %gate.1 = bf16[4,64,8192]{2,1,0:T(8,128)(2,1)} custom-call(s32[1]{0:T(128)S(6)} %copy.70.refs_4_.place_ref, bf16[4,64,8192]{2,1,0:T(8,128)(2,1)} %get-tuple-element.716.query_ref, bf16[8,4,2,64,256]{4,3,2,1,0:T(8,128)(2,1)S(1)} %all-to-all-done.3.refs_0_), custom_call_target="tpu_custom_call", output_to_operand_aliasing={{}: (1, {})} | custom-call | flops 1048576 | bytes 6291456 | tf_op jit(solution)/shard_map/while/body/gate/pallas_call | solution.py:326
  198.2 3.4 %half_gate.1.queries_ref = bf16[4,64,8192]{2,1,0:T(8,128)(2,1)} custom-call(s32[1]{0:T(128)} %bitcast.place_ref, bf16[4,64,8192]{2,1,0:T(8,128)(2,1)} %get-tuple-element.257.queries_ref, bf16[8,2,64,256]{3,2,1,0:T(8,128)(2,1)} %get-tuple-element.748, bf16[8,2,64,256]{3,2,1,0:T(8,128)(2,1)} %collective-permute-done.10.refs_1_), custom_call_target="tpu_custom_call", output_to_operand_aliasing={{}: (1, {})} | custom-call | flops 524288 | bytes 3145728 | tf_op jit(solution)/shard_map/half_gate/pallas_call | solution.py:385
  (36 shorter events, 31.7 us)
Async XLA Ops:
  1.9 15.7 %collective-permute-start = (bf16[4,2,3,8192]{3,1,2,0:T(2,128)(2,1)S(1)}, bf16[4,2,3,8192]{3,1,2,0:T(2,128)(2,1)S(1)}, u32[]{:S(2)}, u32[]{:S(2)}) collective-permute-start(bf16[4,2,3,8192]{3,1,2,0:T(2,128)(2,1)S(1)} %slice.3), channel_id=1, source_target_pairs={{0,1},{1,2},{2,3},{3,4},{4,5},{5,6},{6,7},{7,8},{8,9},{9,10},{10,1... | collective-permute-start | bytes 1179656 | tf_op jit(solution)/shard_map/ppermute | solution.py:18
  22.7 45.4 %collective-permute-start.1 = (bf16[8,2,64,256]{3,2,1,0:T(8,128)(2,1)}, bf16[8,2,64,256]{3,2,1,0:T(8,128)(2,1)}, u32[]{:S(2)}, u32[]{:S(2)}) collective-permute-start(bf16[8,2,64,256]{3,2,1,0:T(8,128)(2,1)} %get-tuple-element.245), channel_id=1, source_target_pairs={{0,24},{8,16},{16,8},{24,0},{1,25},{9,17},{17,9},{25,1},{2,26},{10... | collective-permute-start | bytes 1572872 | tf_op jit(solution)/shard_map/ppermute | solution.py:449
  24.2 46.2 %collective-permute-start.2 = (bf16[8,2,64,256]{3,2,1,0:T(8,128)(2,1)S(1)}, bf16[8,2,64,256]{3,2,1,0:T(8,128)(2,1)}, u32[]{:S(2)}, u32[]{:S(2)}) collective-permute-start(bf16[8,2,64,256]{3,2,1,0:T(8,128)(2,1)S(1)} %get-tuple-element.246), channel_id=1, source_target_pairs={{0,16},{8,24},{16,0},{24,8},{1,17},{9,25},{17,1},{25,9},{2,18},{10... | collective-permute-start | bytes 1572872 | tf_op jit(solution)/shard_map/ppermute | solution.py:449
  25.5 45.0 %collective-permute-start.3 = (bf16[8,2,64,256]{3,2,1,0:T(8,128)(2,1)S(1)}, bf16[8,2,64,256]{3,2,1,0:T(8,128)(2,1)}, u32[]{:S(2)}, u32[]{:S(2)}) collective-permute-start(bf16[8,2,64,256]{3,2,1,0:T(8,128)(2,1)S(1)} %get-tuple-element.247), channel_id=1, source_target_pairs={{0,8},{8,0},{16,24},{24,16},{1,9},{9,1},{17,25},{25,17},{2,10},{10... | collective-permute-start | bytes 1572872 | tf_op jit(solution)/shard_map/ppermute | solution.py:449
  33.5 30.2 %all-to-all-start = ((bf16[8,4,2,64,256]{4,3,2,1,0:T(8,128)(2,1)}), bf16[8,4,2,64,256]{4,3,2,1,0:T(8,128)(2,1)S(1)}, u32[]{:S(2)}, u32[]{:S(2)}) async-start(bf16[8,4,2,64,256]{4,3,2,1,0:T(8,128)(2,1)} %products.3), calls=%async_computation | async-start | bytes 4194304 | tf_op jit(solution)/shard_map/while/body/all_to_all | solution.py:455
  65.1 48.0 %collective-permute-start.7 = (bf16[8,2,64,256]{3,2,1,0:T(8,128)(2,1)}, bf16[8,2,64,256]{3,2,1,0:T(8,128)(2,1)}, u32[]{:S(2)}, u32[]{:S(2)}) collective-permute-start(bf16[8,2,64,256]{3,2,1,0:T(8,128)(2,1)} %get-tuple-element.253), channel_id=1, source_target_pairs={{0,8},{8,0},{16,24},{24,16},{1,9},{9,1},{17,25},{25,17},{2,10},{10... | collective-permute-start | bytes 1572872 | tf_op jit(solution)/shard_map/ppermute | solution.py:449
  65.9 47.7 %collective-permute-start.8 = (bf16[8,2,64,256]{3,2,1,0:T(8,128)(2,1)}, bf16[8,2,64,256]{3,2,1,0:T(8,128)(2,1)}, u32[]{:S(2)}, u32[]{:S(2)}) collective-permute-start(bf16[8,2,64,256]{3,2,1,0:T(8,128)(2,1)} %get-tuple-element.254), channel_id=1, source_target_pairs={{0,16},{8,24},{16,0},{24,8},{1,17},{9,25},{17,1},{25,9},{2,18},{10... | collective-permute-start | bytes 1572872 | tf_op jit(solution)/shard_map/ppermute | solution.py:449
  68.0 48.4 %collective-permute-start.9 = (bf16[8,2,64,256]{3,2,1,0:T(8,128)(2,1)}, bf16[8,2,64,256]{3,2,1,0:T(8,128)(2,1)}, u32[]{:S(2)}, u32[]{:S(2)}) collective-permute-start(bf16[8,2,64,256]{3,2,1,0:T(8,128)(2,1)} %get-tuple-element.255), channel_id=1, source_target_pairs={{0,24},{8,16},{16,8},{24,0},{1,25},{9,17},{17,9},{25,1},{2,26},{10... | collective-permute-start | bytes 1572872 | tf_op jit(solution)/shard_map/ppermute | solution.py:449
  70.5 32.8 %copy-start.1 = (f32[16,1,2048]{2,1,0:T(1,128)S(1)}, f32[16,1,2048]{2,1,0:T(1,128)}, u32[]{:S(2)}) copy-start(f32[16,1,2048]{2,1,0:T(1,128)} %get-tuple-element.667.refs_1_) | copy-start | bytes 393220 | tf_op jit(solution)/shard_map/while
  73.1 30.2 %all-to-all-start.1 = ((bf16[8,4,2,64,256]{4,3,2,1,0:T(8,128)(2,1)}), bf16[8,4,2,64,256]{4,3,2,1,0:T(8,128)(2,1)S(1)}, u32[]{:S(2)}, u32[]{:S(2)}) async-start(bf16[8,4,2,64,256]{4,3,2,1,0:T(8,128)(2,1)} %join.2), calls=%async_computation.1 | async-start | bytes 4194304 | tf_op jit(solution)/shard_map/while/body/all_to_all | solution.py:455
  109.5 49.3 %collective-permute-start.4 = (bf16[8,2,64,256]{3,2,1,0:T(8,128)(2,1)}, bf16[8,2,64,256]{3,2,1,0:T(8,128)(2,1)}, u32[]{:S(2)}, u32[]{:S(2)}) collective-permute-start(bf16[8,2,64,256]{3,2,1,0:T(8,128)(2,1)} %get-tuple-element.250), channel_id=1, source_target_pairs={{0,8},{8,0},{16,24},{24,16},{1,9},{9,1},{17,25},{25,17},{2,10},{10... | collective-permute-start | bytes 1572872 | tf_op jit(solution)/shard_map/ppermute | solution.py:449
  112.1 47.2 %collective-permute-start.5 = (bf16[8,2,64,256]{3,2,1,0:T(8,128)(2,1)}, bf16[8,2,64,256]{3,2,1,0:T(8,128)(2,1)}, u32[]{:S(2)}, u32[]{:S(2)}) collective-permute-start(bf16[8,2,64,256]{3,2,1,0:T(8,128)(2,1)} %get-tuple-element.251), channel_id=1, source_target_pairs={{0,16},{8,24},{16,0},{24,8},{1,17},{9,25},{17,1},{25,9},{2,18},{10... | collective-permute-start | bytes 1572872 | tf_op jit(solution)/shard_map/ppermute | solution.py:449
  113.1 48.3 %collective-permute-start.6 = (bf16[8,2,64,256]{3,2,1,0:T(8,128)(2,1)}, bf16[8,2,64,256]{3,2,1,0:T(8,128)(2,1)}, u32[]{:S(2)}, u32[]{:S(2)}) collective-permute-start(bf16[8,2,64,256]{3,2,1,0:T(8,128)(2,1)} %get-tuple-element.252), channel_id=1, source_target_pairs={{0,24},{8,16},{16,8},{24,0},{1,25},{9,17},{17,9},{25,1},{2,26},{10... | collective-permute-start | bytes 1572872 | tf_op jit(solution)/shard_map/ppermute | solution.py:449
  122.9 1.3 copy-start
  124.2 30.2 %all-to-all-start.2 = ((bf16[8,4,2,64,256]{4,3,2,1,0:T(8,128)(2,1)}), bf16[8,4,2,64,256]{4,3,2,1,0:T(8,128)(2,1)S(1)}, u32[]{:S(2)}, u32[]{:S(2)}) async-start(bf16[8,4,2,64,256]{4,3,2,1,0:T(8,128)(2,1)} %copy-done), calls=%async_computation.2 | async-start | bytes 4194304 | tf_op jit(solution)/shard_map/while/body/all_to_all | solution.py:455
  155.8 42.4 %collective-permute-start.10 = (bf16[8,2,64,256]{3,2,1,0:T(8,128)(2,1)}, bf16[8,2,64,256]{3,2,1,0:T(8,128)(2,1)}, u32[]{:S(2)}, u32[]{:S(2)}) collective-permute-start(bf16[8,2,64,256]{3,2,1,0:T(8,128)(2,1)} %get-tuple-element.258), channel_id=1, source_target_pairs={{0,8},{8,0},{16,24},{24,16},{1,9},{9,1},{17,25},{25,17},{2,10},{10... | collective-permute-start | bytes 1572872 | tf_op jit(solution)/shard_map/ppermute | solution.py:449
  155.9 45.7 %collective-permute-start.11 = (bf16[8,2,64,256]{3,2,1,0:T(8,128)(2,1)}, bf16[8,2,64,256]{3,2,1,0:T(8,128)(2,1)S(1)}, u32[]{:S(2)}, u32[]{:S(2)}) collective-permute-start(bf16[8,2,64,256]{3,2,1,0:T(8,128)(2,1)} %get-tuple-element.259), channel_id=1, source_target_pairs={{0,16},{8,24},{16,0},{24,8},{1,17},{9,25},{17,1},{25,9},{2,18},{10... | collective-permute-start | bytes 1572872 | tf_op jit(solution)/shard_map/ppermute | solution.py:449
  158.8 46.9 %collective-permute-start.12 = (bf16[8,2,64,256]{3,2,1,0:T(8,128)(2,1)}, bf16[8,2,64,256]{3,2,1,0:T(8,128)(2,1)S(1)}, u32[]{:S(2)}, u32[]{:S(2)}) collective-permute-start(bf16[8,2,64,256]{3,2,1,0:T(8,128)(2,1)} %get-tuple-element.260), channel_id=1, source_target_pairs={{0,24},{8,16},{16,8},{24,0},{1,25},{9,17},{17,9},{25,1},{2,26},{10... | collective-permute-start | bytes 1572872 | tf_op jit(solution)/shard_map/ppermute | solution.py:449
  164.0 30.2 %all-to-all-start.3 = ((bf16[8,4,2,64,256]{4,3,2,1,0:T(8,128)(2,1)}), bf16[8,4,2,64,256]{4,3,2,1,0:T(8,128)(2,1)S(1)}, u32[]{:S(2)}, u32[]{:S(2)}) async-start(bf16[8,4,2,64,256]{4,3,2,1,0:T(8,128)(2,1)} %join.3), calls=%async_computation.3 | async-start | bytes 4194304 | tf_op jit(solution)/shard_map/while/body/all_to_all | solution.py:455

commit v4 on v3

--- a/solution.py
+++ b/solution.py
@@ -33,20 +33,22 @@
     return total
 
 
-def product_kernel(place_ref, *refs, seq, outs):
-    if outs == 1:
-        product_body(place_ref[0], *refs, seq=seq, outs=outs)
+def product_kernel(place_ref, *refs, seq, steps):
+    if steps is None:
+        product_body(place_ref[0], *refs, seq=seq, steps=steps)
         return
     for home in range(seq):
-        pl.when(place_ref[0] == home)(functools.partial(product_body, home, *refs, seq=seq, outs=outs))
-
-
-def product_body(place, key_ref, value_ref, key_rim, value_rim, taps_ref, *refs, seq, outs):
-    shifted, outs = refs[-1], refs[-1 - outs : -1]
+        pl.when(place_ref[0] == home)(functools.partial(product_body, home, *refs, seq=seq, steps=steps))
+
+
+def product_body(place, key_ref, value_ref, key_rim, value_rim, taps_ref, *refs, seq, steps):
+    shifted, outs = refs[-1], refs[-1 - (1 if steps is None else len(steps)) : -1]
     count, width = key_ref.shape[0], outs[0].shape[-1]
     spans, lane = key_ref.shape[-1] // (seq * width), shifted.shape[-1]
     for span in range(spans):
         for part in range(seq):
+            if steps is not None and place ^ part not in steps:
+                continue
             for low in range(0, width, lane):
                 start = (span * seq + part) * width + low
                 lanes = slice(start, start + lane)
@@ -57,13 +59,13 @@
                         shifted.at[2 * n + 1], value_ref[n, 0, :, lanes], value_rim[n, 0, :, lanes], value_taps
                     )
                     product = (keys * values).astype(jnp.bfloat16)
-                    if len(outs) == 1:
+                    if steps is None:
                         outs[0][span, place ^ part, n, :, low : low + lane] = product
                     else:
-                        outs[place ^ part][span, n, :, low : low + lane] = product
-
-
-def products(place, proj, rim, taps, first, count, seq, ch, joined, after=()):
+                        outs[steps.index(place ^ part)][span, n, :, low : low + lane] = product
+
+
+def products(place, proj, rim, taps, first, count, seq, ch, steps=None, after=()):
     rows, channels = proj.shape[2:]
     width = channels // (ch * seq)
     spans = math.gcd(ch, 8)
@@ -72,14 +74,14 @@
     def of(component, depth):
         return pl.BlockSpec((1, 1, depth, block), lambda n, j, *_: (first + n, component, 0, j))
 
-    if joined:
+    if steps is None:
         out_specs = [pl.BlockSpec((spans, seq, 1, rows, width), lambda n, j, *_: (j, 0, n, 0, 0))]
         out_shape = [jax.ShapeDtypeStruct((ch, seq, count, rows, width), jnp.bfloat16)]
     else:
-        out_specs = [pl.BlockSpec((spans, 1, rows, width), lambda n, j, *_: (j, n, 0, 0))] * seq
-        out_shape = [jax.ShapeDtypeStruct((ch, count, rows, width), jnp.bfloat16)] * seq
-    return pl.pallas_call(
-        functools.partial(product_kernel, seq=seq, outs=len(out_shape)),
+        out_specs = [pl.BlockSpec((spans, 1, rows, width), lambda n, j, *_: (j, n, 0, 0))] * len(steps)
+        out_shape = [jax.ShapeDtypeStruct((ch, count, rows, width), jnp.bfloat16)] * len(steps)
+    return pl.pallas_call(
+        functools.partial(product_kernel, seq=seq, steps=steps),
         grid_spec=pltpu.PrefetchScalarGridSpec(
             num_scalar_prefetch=1,
             grid=(count, ch // spans),
@@ -468,6 +470,14 @@
     )()
 
 
+def ordered(pieces, order):
+    return [pieces[place] for place in order]
+
+
+def back(pieces, order):
+    return [pieces[order.index(place)] for place in range(len(order))]
+
+
 def staged(times, place, step, *arrays):
     def round_of(_, held):
         return held[0] + 1, *step(held[0], *held[1:])
@@ -488,23 +498,24 @@
     own = lax.dynamic_slice_in_dim(long_filter, place[0] * groups, groups, 0)
     filters = own.astype(jnp.float32).reshape(groups, 1, length)
 
-    first = products(place, turned, rim, taps, 0, half, seq, ch, False)
+    first = products(place, turned, rim, taps, 0, half, seq, ch, tuple(range(1, seq)))
     begun = first[0]
 
     def second_out(place, *held):
-        (second,) = products(place, turned, rim, taps, half, half, seq, ch, True, after=[begun, place])
+        (second,) = products(place, turned, rim, taps, half, half, seq, ch, after=[begun, place])
         queries = short_queries(turned, rim, taps, ch, after=[place])
-        return queries, *split(spread(second))
+        (stays,) = products(place, turned, rim, taps, 0, half, seq, ch, (0,), after=[begun])
+        return queries, stays, *split(spread(second))
 
     shape = jax.ShapeDtypeStruct((seq_count, rows, proj.shape[3]), proj.dtype)
-    queries, *second = staged(once, place, second_out, *vacant(shape, *first))
+    queries, stays, *second = staged(once, place, second_out, *vacant(shape, begun, begun, *first))
     second_sent = second[0]
 
     def first_turn(place, *first):
-        whole = spread(join(first[::-1], after=[place, second_sent]))
-        return long_conv(place, [whole], filters, seq)[::-1]
-
-    first = staged(once, place, first_turn, *swap(first)[::-1])[::-1]
+        whole = spread(join(back(first, [1, 3, 2, 0]), after=[place, second_sent]))
+        return ordered(long_conv(place, [whole], filters, seq), [1, 3, 2, 0])
+
+    first = back(staged(once, place, first_turn, *ordered(swap([stays, *first]), [1, 3, 2, 0])), [1, 3, 2, 0])
     first_sent = first[0]
 
     def second_turn(place, *second):

time: 209 us -> 209 us (level)
  waiting for transfers between devices: 109 us -> 105 us
  Pallas kernels: 48.2 us -> 50.8 us
    all_to_all x4, waiting for transfers between devices: 100 us -> 96.4 us  [spread(): return lax.all_to_all(whole, 'ch', split_axis=0, concat_axis=0, tiled=True)]
    pallas_call x2 -> x3, Pallas kernels: 10.3 us -> 12 us  [products(): pl.pallas_call(functools.partial(product_kernel, seq=seq, steps=steps), g...]
  transfers between devices with their start and end apart: 17 -> 17, of which waited for: 8 -> 8; matrix products, arithmetic and copies ran while one was open for 1% -> 1% of each run, Pallas kernels for 20% -> 21%
where the time goes in v4:
time: 209 us; the launch traced here: 208 us
  waiting for transfers between devices  105 us (50%)
  Pallas kernels  50.8 us (24%)
  starting transfers between devices  32.3 us (15%)
  blocking collectives  13.8 us (7%)
  local copies, waits for them, and re-layouts  4.52 us (2%)
    all_to_all x4, waiting for transfers between devices, spread(): return lax.all_to_all(whole, 'ch', split_axis=0, concat_axis=0, tiled=True)  96.4 us
    ppermute x12, starting transfers between devices, swap(): lax.ppermute(piece, 'seq', [(source, source ^ step) for source in range(c...  16 us
    all_to_all x4, starting transfers between devices, spread(): return lax.all_to_all(whole, 'ch', split_axis=0, concat_axis=0, tiled=True)  14.4 us
    all_gather x1, blocking collectives, shards(): taps = lax.all_gather(short_w, 'ch', axis=2, tiled=True)  13.8 us
    pallas_call x2, Pallas kernels, long_conv(): pl.pallas_call(functools.partial(conv_kernel, seq=seq, joined=joined), gr...  12.7 us
    pallas_call x3, Pallas kernels, products(): pl.pallas_call(functools.partial(product_kernel, seq=seq, steps=steps), g...  12 us
    ppermute x12, waiting for transfers between devices, swap(): lax.ppermute(piece, 'seq', [(source, source ^ step) for source in range(c...  9.04 us
    pallas_call x1, Pallas kernels, short_queries(): pl.pallas_call(queries_kernel, grid=(channels // block,), in_specs=[of(ro...  6.9 us
  transfers between devices with their start and end apart: 17, of which 8 were waited for; matrix products, arithmetic and copies ran while one was open for 1% of the time, Pallas kernels for 21%

profile of v4, /device:TPU:8, one launch (start us, length us, event | category | flops | bytes accessed | tf_op | source)
XLA Modules:
  0.0 207.9 jit_solution(13171930496417114125)
XLA Ops:
  3.8 13.8 %all_gather.3.refs_4_ = f32[3,3,8192]{2,1,0:T(4,128)} all-gather(f32[3,3,1024]{2,1,0:T(4,128)} %param.12), channel_id=1, replica_groups=mesh['seq'=4,'ch'=8] {'ch'}, dimensions={2}, use_global_device_ids=true | all-gather | bytes 331776 | tf_op jit(solution)/shard_map/all_gather | solution.py:496
  17.6 4.3 %products.3 = (bf16[8,2,64,256]{3,2,1,0:T(8,128)(2,1)}, bf16[8,2,64,256]{3,2,1,0:T(8,128)(2,1)S(1)}, bf16[8,2,64,256]{3,2,1,0:T(8,128)(2,1)S(1)}) custom-call(s32[1]{0:T(128)} %bitcast.place_ref, bf16[4,3,64,8192]{3,2,1,0:T(8,128)(2,1)} %bitcast.3, bf16[4,3,64,8192]{3,2,1,0:T(8,128)(2,1)} %bitcast.4, bf16[4,3,2,8192]{3,2,1,0:T(2,128)(2,1)S(1)} %bitcast.6, ...), custom_call_target="tpu_custom_call" | custom-call | flops 20971520 | bytes 6291456 | tf_op jit(solution)/shard_map/products/pallas_call | solution.py:83
  22.4 2.7 %collective-permute-start.2 = (bf16[8,2,64,256]{3,2,1,0:T(8,128)(2,1)S(1)}, bf16[8,2,64,256]{3,2,1,0:T(8,128)(2,1)}, u32[]{:S(2)}, u32[]{:S(2)}) collective-permute-start(bf16[8,2,64,256]{3,2,1,0:T(8,128)(2,1)S(1)} %get-tuple-element.251), channel_id=1, source_target_pairs={{0,24},{8,16},{16,8},{24,0},{1,25},{9,17},{17,9},{25,1},{2,26},{10... | collective-permute-start | bytes 1572872 | tf_op jit(solution)/shard_map/ppermute | solution.py:451
  27.9 36.9 %while.70 = (s32[]{:T(128)}, s32[1]{0:T(128)}, bf16[4,64,8192]{2,1,0:T(8,128)(2,1)}, bf16[8,2,64,256]{3,2,1,0:T(8,128)(2,1)}, bf16[8,2,64,256]{3,2,1,0:T(8,128)(...) while((s32[]{:T(128)}, s32[1]{0:T(128)}, ...), condition=%wide.region_1.0_spmd, body=%wide.region_0.0_spmd.sunk | while | flops 58720256 | bytes 81789152 | solution.py:485
  27.9 5.2 %products.5 = bf16[8,4,2,64,256]{4,3,2,1,0:T(8,128)(2,1)} custom-call(s32[1]{0:T(128)S(6)} %copy.18.refs_0_.place_ref.refs_6_, bf16[4,3,64,8192]{3,2,1,0:T(8,128)(2,1)} %get-tuple-element.646.query_ref.refs_0_.refs_1_, bf16[4,3,64,8192]{3,2,1,0:T(8,128)(2,1)} %get-tuple-element.646.query_ref.refs_0_.refs_1_, ...), custom_call_target="tpu_custom_call" | custom-call | flops 20971520 | bytes 6291456 | tf_op jit(solution)/shard_map/while/body/products/pallas_call | solution.py:83
  33.1 3.6 %all-to-all-start = ((bf16[8,4,2,64,256]{4,3,2,1,0:T(8,128)(2,1)}), bf16[8,4,2,64,256]{4,3,2,1,0:T(8,128)(2,1)S(1)}, u32[]{:S(2)}, u32[]{:S(2)}) async-start(bf16[8,4,2,64,256]{4,3,2,1,0:T(8,128)(2,1)} %products.5), calls=%async_computation | async-start | bytes 4194304 | tf_op jit(solution)/shard_map/while/body/all_to_all | solution.py:457
  36.7 6.9 %queries.1 = bf16[4,64,8192]{2,1,0:T(8,128)(2,1)} custom-call(bf16[4,3,64,8192]{3,2,1,0:T(8,128)(2,1)} %get-tuple-element.646.query_ref.refs_0_.refs_1_, bf16[4,3,2,8192]{3,2,1,0:T(2,128)(2,1)S(1)} %get-tuple-element.647.query_rim.refs_2_.refs_3_, f32[3,3,8192]{2,1,0:T(4,128)} %get-tuple-element.648.query_taps.refs_4_, s32[1]{0:T(128)S(6)} %copy.18.refs_0_.place_ref.refs_6_), custom_call_target="tpu_custom_call" | custom-call | flops 16777216 | bytes 8388608 | tf_op jit(solution)/shard_map/while/body/queries/pallas_call | solution.py:121
  46.7 16.6 %all-to-all-done.whole_ref = bf16[8,4,2,64,256]{4,3,2,1,0:T(8,128)(2,1)S(1)} async-done(((bf16[8,4,2,64,256]{4,3,2,1,0:T(8,128)(2,1)}), bf16[8,4,2,64,256]{4,3,2,1,0:T(8,128)(2,1)S(1)}, u32[]{:S(2)}, u32[]{:S(2)}) %all-to-all-start) | async-done | bytes 2097184 | tf_op jit(solution)/shard_map/while/body/all_to_all | solution.py:457
  65.0 2.8 %collective-permute-start.8 = (bf16[8,2,64,256]{3,2,1,0:T(8,128)(2,1)}, bf16[8,2,64,256]{3,2,1,0:T(8,128)(2,1)}, u32[]{:S(2)}, u32[]{:S(2)}) collective-permute-start(bf16[8,2,64,256]{3,2,1,0:T(8,128)(2,1)} %get-tuple-element.260), channel_id=1, source_target_pairs={{0,16},{8,24},{16,0},{24,8},{1,17},{9,25},{17,1},{25,9},{2,18},{10... | collective-permute-start | bytes 1572872 | tf_op jit(solution)/shard_map/ppermute | solution.py:451
  68.3 2.8 %collective-permute-done.3 = bf16[8,2,64,256]{3,2,1,0:T(8,128)(2,1)} collective-permute-done((bf16[8,2,64,256]{3,2,1,0:T(8,128)(2,1)S(1)}, bf16[8,2,64,256]{3,2,1,0:T(8,128)(2,1)}, u32[]{:S(2)}, u32[]{:S(2)}) %collective-permute-start.3) | collective-permute-done | bytes 524320 | tf_op jit(solution)/shard_map/ppermute | solution.py:451
  71.0 39.1 %while.71 = (s32[]{:T(128)}, s32[1]{0:T(128)}, bf16[8,2,64,256]{3,2,1,0:T(8,128)(2,1)}, bf16[8,2,64,256]{3,2,1,0:T(8,128)(2,1)}, bf16[8,2,64,256]{3,2,1,0:T(8,12...) while((s32[]{:T(128)}, s32[1]{0:T(128)}, ...), condition=%wide.region_3.0_spmd, body=%wide.region_2.0_spmd.sunk | while | flops 2415919104 | bytes 15204541 | solution.py:485
  73.7 3.6 %all-to-all-start.1 = ((bf16[8,4,2,64,256]{4,3,2,1,0:T(8,128)(2,1)}), bf16[8,4,2,64,256]{4,3,2,1,0:T(8,128)(2,1)S(1)}, u32[]{:S(2)}, u32[]{:S(2)}) async-start(bf16[8,4,2,64,256]{4,3,2,1,0:T(8,128)(2,1)} %join.2), calls=%async_computation.1 | async-start | bytes 4194304 | tf_op jit(solution)/shard_map/while/body/all_to_all | solution.py:457
  77.3 26.6 %all-to-all-done.1.refs_0_ = bf16[8,4,2,64,256]{4,3,2,1,0:T(8,128)(2,1)S(1)} async-done(((bf16[8,4,2,64,256]{4,3,2,1,0:T(8,128)(2,1)}), bf16[8,4,2,64,256]{4,3,2,1,0:T(8,128)(2,1)S(1)}, u32[]{:S(2)}, u32[]{:S(2)}) %all-to-all-start.1) | async-done | bytes 2097184 | tf_op jit(solution)/shard_map/while/body/all_to_all | solution.py:457
  103.9 6.2 %long_conv.2 = (bf16[8,2,64,256]{3,2,1,0:T(8,128)(2,1)}, bf16[8,2,64,256]{3,2,1,0:T(8,128)(2,1)}, bf16[8,2,64,256]{3,2,1,0:T(8,128)(2,1)}, bf16[8,2,64,256]{3,2,1,0:T(8,128)(2,1)}) custom-call(s32[1]{0:T(128)S(6)} %copy.40.refs_4_.place_ref, bf16[8,4,2,64,256]{4,3,2,1,0:T(8,128)(2,1)S(1)} %all-to-all-done.1.refs_0_, f32[16,1,2048]{2,1,0:T(1,128)S(1)} %copy-done.2), custom_call_target="tpu_custom_call" | custom-call | flops 2415919104 | bytes 4194304 | tf_op jit(solution)/shard_map/while/body/long_conv/pallas_call | solution.py:232
  116.6 39.4 %while.72 = (s32[]{:T(128)}, s32[1]{0:T(128)}, bf16[8,2,64,256]{3,2,1,0:T(8,128)(2,1)}, bf16[8,2,64,256]{3,2,1,0:T(8,128)(2,1)}, bf16[8,2,64,256]{3,2,1,0:T(8,12...) while((s32[]{:T(128)}, s32[1]{0:T(128)}, ...), condition=%wide.region_5.0_spmd, body=%wide.region_4.0_spmd.sunk | while | flops 2415919104 | bytes 23068852 | solution.py:485
  116.6 6.5 %long_conv.3 = bf16[8,4,2,64,256]{4,3,2,1,0:T(8,128)(2,1)S(1)} custom-call(s32[1]{0:T(128)} %get-tuple-element.697.place_ref, bf16[8,2,64,256]{3,2,1,0:T(8,128)(2,1)} %get-tuple-element.698.refs_0_, bf16[8,2,64,256]{3,2,1,0:T(8,128)(2,1)} %get-tuple-element.699.refs_1_, bf16[8,2,64,256]{3,2,1,0:T(8,128)(2,1)} %get-tuple-element.700.refs_2_, ...), custom_call_target="tpu_custom_call" | custom-call | flops 2415919104 | bytes 4194304 | tf_op jit(solution)/shard_map/while/body/long_conv/pallas_call | solution.py:232
  124.4 3.6 %all-to-all-start.2 = ((bf16[8,4,2,64,256]{4,3,2,1,0:T(8,128)(2,1)}), bf16[8,4,2,64,256]{4,3,2,1,0:T(8,128)(2,1)S(1)}, u32[]{:S(2)}, u32[]{:S(2)}) async-start(bf16[8,4,2,64,256]{4,3,2,1,0:T(8,128)(2,1)} %copy-done), calls=%async_computation.2 | async-start | bytes 4194304 | tf_op jit(solution)/shard_map/while/body/all_to_all | solution.py:457
  128.0 26.6 %all-to-all-done.2.whole_ref = bf16[8,4,2,64,256]{4,3,2,1,0:T(8,128)(2,1)S(1)} async-done(((bf16[8,4,2,64,256]{4,3,2,1,0:T(8,128)(2,1)}), bf16[8,4,2,64,256]{4,3,2,1,0:T(8,128)(2,1)S(1)}, u32[]{:S(2)}, u32[]{:S(2)}) %all-to-all-start.2) | async-done | bytes 2097184 | tf_op jit(solution)/shard_map/while/body/all_to_all | solution.py:457
  156.1 3.5 %collective-permute-start.11 = (bf16[8,2,64,256]{3,2,1,0:T(8,128)(2,1)}, bf16[8,2,64,256]{3,2,1,0:T(8,128)(2,1)S(1)}, u32[]{:S(2)}, u32[]{:S(2)}) collective-permute-start(bf16[8,2,64,256]{3,2,1,0:T(8,128)(2,1)} %get-tuple-element.265), channel_id=1, source_target_pairs={{0,16},{8,24},{16,0},{24,8},{1,17},{9,25},{17,1},{25,9},{2,18},{10... | collective-permute-start | bytes 1572872 | tf_op jit(solution)/shard_map/ppermute | solution.py:451
  161.6 36.8 %while.73 = (s32[]{:T(128)}, s32[1]{0:T(128)}, bf16[4,64,8192]{2,1,0:T(8,128)(2,1)}, s32[]{:T(128)}, bf16[8,2,64,256]{3,2,1,0:T(8,128)(2,1)}, /*index=5*/bf16[8,...) while((s32[]{:T(128)}, s32[1]{0:T(128)}, ...), condition=%wide.region_7.0_spmd, body=%wide.region_6.0_spmd.sunk | while | flops 1048579 | bytes 16777376 | solution.py:485
  164.2 3.6 %all-to-all-start.3 = ((bf16[8,4,2,64,256]{4,3,2,1,0:T(8,128)(2,1)}), bf16[8,4,2,64,256]{4,3,2,1,0:T(8,128)(2,1)S(1)}, u32[]{:S(2)}, u32[]{:S(2)}) async-start(bf16[8,4,2,64,256]{4,3,2,1,0:T(8,128)(2,1)} %join.3), calls=%async_computation.3 | async-start | bytes 4194304 | tf_op jit(solution)/shard_map/while/body/all_to_all | solution.py:457
  167.8 26.6 %all-to-all-done.3.refs_0_ = bf16[8,4,2,64,256]{4,3,2,1,0:T(8,128)(2,1)S(1)} async-done(((bf16[8,4,2,64,256]{4,3,2,1,0:T(8,128)(2,1)}), bf16[8,4,2,64,256]{4,3,2,1,0:T(8,128)(2,1)S(1)}, u32[]{:S(2)}, u32[]{:S(2)}) %all-to-all-start.3) | async-done | bytes 2097184 | tf_op jit(solution)/shard_map/while/body/all_to_all | solution.py:457
  194.4 4.0 %gate.1 = bf16[4,64,8192]{2,1,0:T(8,128)(2,1)} custom-call(s32[1]{0:T(128)S(6)} %copy.73.refs_4_.place_ref, bf16[4,64,8192]{2,1,0:T(8,128)(2,1)} %get-tuple-element.731.query_ref, bf16[8,4,2,64,256]{4,3,2,1,0:T(8,128)(2,1)S(1)} %all-to-all-done.3.refs_0_), custom_call_target="tpu_custom_call", output_to_operand_aliasing={{}: (1, {})} | custom-call | flops 1048576 | bytes 6291456 | tf_op jit(solution)/shard_map/while/body/gate/pallas_call | solution.py:328
  198.3 3.4 %half_gate.1.queries_ref = bf16[4,64,8192]{2,1,0:T(8,128)(2,1)} custom-call(s32[1]{0:T(128)} %bitcast.place_ref, bf16[4,64,8192]{2,1,0:T(8,128)(2,1)} %get-tuple-element.263.queries_ref, bf16[8,2,64,256]{3,2,1,0:T(8,128)(2,1)} %get-tuple-element.763, bf16[8,2,64,256]{3,2,1,0:T(8,128)(2,1)} %collective-permute-done.10.refs_1_), custom_call_target="tpu_custom_call", output_to_operand_aliasing={{}: (1, {})} | custom-call | flops 524288 | bytes 3145728 | tf_op jit(solution)/shard_map/half_gate/pallas_call | solution.py:387
  (39 shorter events, 34.9 us)
Async XLA Ops:
  1.9 15.7 %collective-permute-start = (bf16[4,2,3,8192]{3,1,2,0:T(2,128)(2,1)S(1)}, bf16[4,2,3,8192]{3,1,2,0:T(2,128)(2,1)S(1)}, u32[]{:S(2)}, u32[]{:S(2)}) collective-permute-start(bf16[4,2,3,8192]{3,1,2,0:T(2,128)(2,1)S(1)} %slice.3), channel_id=1, source_target_pairs={{0,1},{1,2},{2,3},{3,4},{4,5},{5,6},{6,7},{7,8},{8,9},{9,10},{10,1... | collective-permute-start | bytes 1179656 | tf_op jit(solution)/shard_map/ppermute | solution.py:18
  21.9 45.9 %collective-permute-start.1 = (bf16[8,2,64,256]{3,2,1,0:T(8,128)(2,1)}, bf16[8,2,64,256]{3,2,1,0:T(8,128)(2,1)}, u32[]{:S(2)}, u32[]{:S(2)}) collective-permute-start(bf16[8,2,64,256]{3,2,1,0:T(8,128)(2,1)} %get-tuple-element.619), channel_id=1, source_target_pairs={{0,8},{8,0},{16,24},{24,16},{1,9},{9,1},{17,25},{25,17},{2,10},{10... | collective-permute-start | bytes 1572872 | tf_op jit(solution)/shard_map/ppermute | solution.py:451
  22.4 45.9 %collective-permute-start.2 = (bf16[8,2,64,256]{3,2,1,0:T(8,128)(2,1)S(1)}, bf16[8,2,64,256]{3,2,1,0:T(8,128)(2,1)}, u32[]{:S(2)}, u32[]{:S(2)}) collective-permute-start(bf16[8,2,64,256]{3,2,1,0:T(8,128)(2,1)S(1)} %get-tuple-element.251), channel_id=1, source_target_pairs={{0,24},{8,16},{16,8},{24,0},{1,25},{9,17},{17,9},{25,1},{2,26},{10... | collective-permute-start | bytes 1572872 | tf_op jit(solution)/shard_map/ppermute | solution.py:451
  25.1 46.0 %collective-permute-start.3 = (bf16[8,2,64,256]{3,2,1,0:T(8,128)(2,1)S(1)}, bf16[8,2,64,256]{3,2,1,0:T(8,128)(2,1)}, u32[]{:S(2)}, u32[]{:S(2)}) collective-permute-start(bf16[8,2,64,256]{3,2,1,0:T(8,128)(2,1)S(1)} %get-tuple-element.252), channel_id=1, source_target_pairs={{0,16},{8,24},{16,0},{24,8},{1,17},{9,25},{17,1},{25,9},{2,18},{10... | collective-permute-start | bytes 1572872 | tf_op jit(solution)/shard_map/ppermute | solution.py:451
  33.1 30.2 %all-to-all-start = ((bf16[8,4,2,64,256]{4,3,2,1,0:T(8,128)(2,1)}), bf16[8,4,2,64,256]{4,3,2,1,0:T(8,128)(2,1)S(1)}, u32[]{:S(2)}, u32[]{:S(2)}) async-start(bf16[8,4,2,64,256]{4,3,2,1,0:T(8,128)(2,1)} %products.5), calls=%async_computation | async-start | bytes 4194304 | tf_op jit(solution)/shard_map/while/body/all_to_all | solution.py:457
  36.7 7.5 %copy-start.1 = (bf16[4,3,64,8192]{3,2,1,0:T(8,128)(2,1)S(1)}, bf16[4,3,64,8192]{3,2,1,0:T(8,128)(2,1)}, u32[]{:S(2)}) copy-start(bf16[4,3,64,8192]{3,2,1,0:T(8,128)(2,1)} %get-tuple-element.646.query_ref.refs_0_.refs_1_) | copy-start | bytes 37748740 | tf_op jit(solution)/shard_map/while
  64.8 49.3 %collective-permute-start.7 = (bf16[8,2,64,256]{3,2,1,0:T(8,128)(2,1)}, bf16[8,2,64,256]{3,2,1,0:T(8,128)(2,1)}, u32[]{:S(2)}, u32[]{:S(2)}) collective-permute-start(bf16[8,2,64,256]{3,2,1,0:T(8,128)(2,1)} %get-tuple-element.259), channel_id=1, source_target_pairs={{0,8},{8,0},{16,24},{24,16},{1,9},{9,1},{17,25},{25,17},{2,10},{10... | collective-permute-start | bytes 1572872 | tf_op jit(solution)/shard_map/ppermute | solution.py:451
  65.0 49.7 %collective-permute-start.8 = (bf16[8,2,64,256]{3,2,1,0:T(8,128)(2,1)}, bf16[8,2,64,256]{3,2,1,0:T(8,128)(2,1)}, u32[]{:S(2)}, u32[]{:S(2)}) collective-permute-start(bf16[8,2,64,256]{3,2,1,0:T(8,128)(2,1)} %get-tuple-element.260), channel_id=1, source_target_pairs={{0,16},{8,24},{16,0},{24,8},{1,17},{9,25},{17,1},{25,9},{2,18},{10... | collective-permute-start | bytes 1572872 | tf_op jit(solution)/shard_map/ppermute | solution.py:451
  67.8 48.8 %collective-permute-start.9 = (bf16[8,2,64,256]{3,2,1,0:T(8,128)(2,1)}, bf16[8,2,64,256]{3,2,1,0:T(8,128)(2,1)}, u32[]{:S(2)}, u32[]{:S(2)}) collective-permute-start(bf16[8,2,64,256]{3,2,1,0:T(8,128)(2,1)} %get-tuple-element.261), channel_id=1, source_target_pairs={{0,24},{8,16},{16,8},{24,0},{1,25},{9,17},{17,9},{25,1},{2,26},{10... | collective-permute-start | bytes 1572872 | tf_op jit(solution)/shard_map/ppermute | solution.py:451
  71.0 32.8 %copy-start.2 = (f32[16,1,2048]{2,1,0:T(1,128)S(1)}, f32[16,1,2048]{2,1,0:T(1,128)}, u32[]{:S(2)}) copy-start(f32[16,1,2048]{2,1,0:T(1,128)} %get-tuple-element.682.refs_1_) | copy-start | bytes 393220 | tf_op jit(solution)/shard_map/while
  73.7 30.2 %all-to-all-start.1 = ((bf16[8,4,2,64,256]{4,3,2,1,0:T(8,128)(2,1)}), bf16[8,4,2,64,256]{4,3,2,1,0:T(8,128)(2,1)S(1)}, u32[]{:S(2)}, u32[]{:S(2)}) async-start(bf16[8,4,2,64,256]{4,3,2,1,0:T(8,128)(2,1)} %join.2), calls=%async_computation.1 | async-start | bytes 4194304 | tf_op jit(solution)/shard_map/while/body/all_to_all | solution.py:457
  110.1 49.5 %collective-permute-start.4 = (bf16[8,2,64,256]{3,2,1,0:T(8,128)(2,1)}, bf16[8,2,64,256]{3,2,1,0:T(8,128)(2,1)}, u32[]{:S(2)}, u32[]{:S(2)}) collective-permute-start(bf16[8,2,64,256]{3,2,1,0:T(8,128)(2,1)} %get-tuple-element.256), channel_id=1, source_target_pairs={{0,8},{8,0},{16,24},{24,16},{1,9},{9,1},{17,25},{25,17},{2,10},{10... | collective-permute-start | bytes 1572872 | tf_op jit(solution)/shard_map/ppermute | solution.py:451
  112.2 47.3 %collective-permute-start.5 = (bf16[8,2,64,256]{3,2,1,0:T(8,128)(2,1)}, bf16[8,2,64,256]{3,2,1,0:T(8,128)(2,1)}, u32[]{:S(2)}, u32[]{:S(2)}) collective-permute-start(bf16[8,2,64,256]{3,2,1,0:T(8,128)(2,1)} %get-tuple-element.257), channel_id=1, source_target_pairs={{0,16},{8,24},{16,0},{24,8},{1,17},{9,25},{17,1},{25,9},{2,18},{10... | collective-permute-start | bytes 1572872 | tf_op jit(solution)/shard_map/ppermute | solution.py:451
  114.1 47.5 %collective-permute-start.6 = (bf16[8,2,64,256]{3,2,1,0:T(8,128)(2,1)}, bf16[8,2,64,256]{3,2,1,0:T(8,128)(2,1)}, u32[]{:S(2)}, u32[]{:S(2)}) collective-permute-start(bf16[8,2,64,256]{3,2,1,0:T(8,128)(2,1)} %get-tuple-element.258), channel_id=1, source_target_pairs={{0,24},{8,16},{16,8},{24,0},{1,25},{9,17},{17,9},{25,1},{2,26},{10... | collective-permute-start | bytes 1572872 | tf_op jit(solution)/shard_map/ppermute | solution.py:451
  123.1 1.4 copy-start
  124.4 30.2 %all-to-all-start.2 = ((bf16[8,4,2,64,256]{4,3,2,1,0:T(8,128)(2,1)}), bf16[8,4,2,64,256]{4,3,2,1,0:T(8,128)(2,1)S(1)}, u32[]{:S(2)}, u32[]{:S(2)}) async-start(bf16[8,4,2,64,256]{4,3,2,1,0:T(8,128)(2,1)} %copy-done), calls=%async_computation.2 | async-start | bytes 4194304 | tf_op jit(solution)/shard_map/while/body/all_to_all | solution.py:457
  156.0 42.3 %collective-permute-start.10 = (bf16[8,2,64,256]{3,2,1,0:T(8,128)(2,1)}, bf16[8,2,64,256]{3,2,1,0:T(8,128)(2,1)}, u32[]{:S(2)}, u32[]{:S(2)}) collective-permute-start(bf16[8,2,64,256]{3,2,1,0:T(8,128)(2,1)} %get-tuple-element.264), channel_id=1, source_target_pairs={{0,8},{8,0},{16,24},{24,16},{1,9},{9,1},{17,25},{25,17},{2,10},{10... | collective-permute-start | bytes 1572872 | tf_op jit(solution)/shard_map/ppermute | solution.py:451
  156.1 45.7 %collective-permute-start.11 = (bf16[8,2,64,256]{3,2,1,0:T(8,128)(2,1)}, bf16[8,2,64,256]{3,2,1,0:T(8,128)(2,1)S(1)}, u32[]{:S(2)}, u32[]{:S(2)}) collective-permute-start(bf16[8,2,64,256]{3,2,1,0:T(8,128)(2,1)} %get-tuple-element.265), channel_id=1, source_target_pairs={{0,16},{8,24},{16,0},{24,8},{1,17},{9,25},{17,1},{25,9},{2,18},{10... | collective-permute-start | bytes 1572872 | tf_op jit(solution)/shard_map/ppermute | solution.py:451
  159.6 46.3 %collective-permute-start.12 = (bf16[8,2,64,256]{3,2,1,0:T(8,128)(2,1)}, bf16[8,2,64,256]{3,2,1,0:T(8,128)(2,1)S(1)}, u32[]{:S(2)}, u32[]{:S(2)}) collective-permute-start(bf16[8,2,64,256]{3,2,1,0:T(8,128)(2,1)} %get-tuple-element.266), channel_id=1, source_target_pairs={{0,24},{8,16},{16,8},{24,0},{1,25},{9,17},{17,9},{25,1},{2,26},{10... | collective-permute-start | bytes 1572872 | tf_op jit(solution)/shard_map/ppermute | solution.py:451
  164.2 30.2 %all-to-all-start.3 = ((bf16[8,4,2,64,256]{4,3,2,1,0:T(8,128)(2,1)}), bf16[8,4,2,64,256]{4,3,2,1,0:T(8,128)(2,1)S(1)}, u32[]{:S(2)}, u32[]{:S(2)}) async-start(bf16[8,4,2,64,256]{4,3,2,1,0:T(8,128)(2,1)} %join.3), calls=%async_computation.3 | async-start | bytes 4194304 | tf_op jit(solution)/shard_map/while/body/all_to_all | solution.py:457
